TPU v7x, 32 devices: a whole 2x2x4 slice. The times are simulated.
32 devices in a mesh: role: 2 (over core), dp: 16 (over z, y, x).
Axes of the slice: x: 2, y: 2, z: 4, core: 2. Of those that a mesh axis runs over, the one named last changes fastest.
Arguments:
- board_now: bfloat16 [1024, 10, 10, 128], P('dp'), may hold values from -6 to 6
- traj_boards: bfloat16 [16, 16, 10, 10, 128], P('dp'), may hold values from -6 to 6
- actions: int32 [16, 16], P('dp'), may hold values from 0 to 399
- lengths: int32 [16], P('dp'), may hold values from 1 to 16, 160 in all
- behaviour: float32 [16, 16], P('dp'), may hold values from -7 to -4.5
- regular: float32 [16, 16], P('dp'), may hold values from -7 to -4.5
- rewards: float32 [16, 16], P('dp'), may hold values from -4 to 4
- torso: float32 [2304, 128], replicated, may hold values from -0.1875 to 0.1875
- policy_head: bfloat16 [128, 4], replicated, may hold values from -0.5 to 0.5
- value_head: bfloat16 [128], replicated, may hold values from -2.390625 to 2.390625
- first_moment: float32 [2304, 128], P('dp'), may hold values from -6 to 6
- second_moment: float32 [2304, 128], P('dp'), may hold values from 0.5 to 2
Outputs:
- new_weights: float32 [2304, 128], P('dp')
- move_logp: float32 [1024, 400], P('dp')
Inputs may be any that keep to these rules, and one draw needn't show every extreme that they name: `lengths`: live moves of a trajectory are its first slots; some trajectory has all 16.
All inputs are finite; a program needn't handle non-finite values. No bound on the sum of `lengths` on one device may be relied on, other than what follows from the above.
Results may differ from a plain program's by a relative error of at most 0.0027.
The roundings to bfloat16 on the way count: a program that leaves them out, or rounds other values in their place, can miss the bound.
Values sent between devices are 32-bit elements; how exact they have to be, the bound alone decides.
A program may use at most 128 MiB of HBM per device.

v0:
```python
import math

import jax
import jax.numpy as jnp
from jax import lax
from jax.sharding import PartitionSpec as P

ETA = 0.2
LEARN_RATE = 0.03
BETA_ONE = 0.9
BETA_TWO = 0.999
ADAM_EPS = 1e-08
NORM_EPS = 1e-12


def from_root(x, axis, root):
    mine = lax.axis_index(axis) == root
    return lax.psum(jnp.where(mine, x, jnp.zeros_like(x)), axis)


def conv_sum(boards, kernel):
    extent = boards.shape[1]
    padded = jnp.pad(boards, ((0, 0), (1, 1), (1, 1), (0, 0)))
    summed = jnp.zeros(boards.shape, jnp.float32)
    for offset in range(9):
        row_start = offset // 3
        col_start = offset % 3
        window = padded[:, row_start : row_start + extent, col_start : col_start + extent, :]
        summed = summed + jnp.dot(window, kernel[offset], preferred_element_type=jnp.float32)
    return summed


def torso_forward(boards, kernels):
    layer_inputs = []
    pre_acts = []
    hidden = boards
    for layer_index in range(kernels.shape[0]):
        pre_act = conv_sum(hidden, kernels[layer_index])
        layer_inputs.append(hidden)
        pre_acts.append(pre_act)
        hidden = (hidden.astype(jnp.float32) + jax.nn.relu(pre_act)).astype(jnp.bfloat16)
    return (hidden, layer_inputs, pre_acts)


def policy_logits(hidden, policy_head):
    per_cell = jnp.dot(hidden, policy_head, preferred_element_type=jnp.float32)
    return jnp.transpose(per_cell, (0, 3, 1, 2)).reshape(hidden.shape[0], -1)


def heads_forward(hidden, policy_head, value_head, actions):
    logits = policy_logits(hidden, policy_head)
    log_total = jnp.log(jnp.sum(jnp.exp(logits), axis=1))
    action_ids = lax.broadcasted_iota(jnp.int32, logits.shape, 1)
    picked = jnp.sum(jnp.where(action_ids == actions[:, None], logits, 0.0), axis=1)
    value_cells = jnp.dot(hidden, value_head, preferred_element_type=jnp.float32)
    value_estimates = jnp.tanh(jnp.mean(value_cells, axis=(1, 2)))
    return (logits, log_total, picked - log_total, value_estimates)


def vee_trace_cotangents(
    policy_log_probs, value_estimates, behaviour, regular, rewards, trajectory_length
):
    positions = jnp.arange(policy_log_probs.shape[0], dtype=jnp.int32)
    live_mask = (positions < trajectory_length).astype(jnp.float32)
    next_live = (positions + 1 < trajectory_length).astype(jnp.float32)
    clipped_ratio = jnp.minimum(1.0, jnp.exp(policy_log_probs - behaviour))
    shaped = rewards - ETA * (policy_log_probs - regular)
    next_values = jnp.concatenate([value_estimates[1:], jnp.zeros((1,), jnp.float32)]) * next_live
    deltas = live_mask * clipped_ratio * (shaped + next_values - value_estimates)

    def backward_step(running, inputs):
        delta_now, ratio_now, live_now = inputs
        correction = live_now * (delta_now + ratio_now * running)
        return (correction, correction)

    _, corrections = lax.scan(
        backward_step, jnp.zeros((), jnp.float32), (deltas, clipped_ratio, live_mask), reverse=True
    )
    targets = value_estimates + corrections
    next_targets = jnp.concatenate([targets[1:], jnp.zeros((1,), jnp.float32)]) * next_live
    policy_gradient_term = -live_mask * clipped_ratio * (shaped + next_targets - value_estimates)
    value_gradient_term = -live_mask * (targets - value_estimates)
    return (policy_gradient_term, value_gradient_term)


def heads_backward(
    board_shape,
    policy_gradient_term,
    value_gradient_term,
    logits,
    log_total,
    value_estimates,
    actions,
    policy_head,
    value_head,
):
    probabilities = jnp.exp(logits - log_total[:, None])
    action_ids = lax.broadcasted_iota(jnp.int32, logits.shape, 1)
    onehot = (action_ids == actions[:, None]).astype(jnp.float32)
    logit_grad = policy_gradient_term[:, None] * (onehot - probabilities)
    row_count = board_shape[0]
    extent = board_shape[1]
    cell_grad = jnp.transpose(logit_grad.reshape(row_count, -1, extent, extent), (0, 2, 3, 1))
    hidden_grad = jnp.dot(
        cell_grad, policy_head.astype(jnp.float32).T, precision=lax.Precision.HIGHEST
    )
    value_cell = value_gradient_term * (1.0 - value_estimates * value_estimates) / (extent * extent)
    return hidden_grad + value_cell[:, None, None, None] * value_head.astype(jnp.float32)


def layer_backward(layer_input, pre_act, out_grad, kernel, need_input):
    extent = layer_input.shape[1]
    channels = layer_input.shape[3]
    act_grad = (out_grad * (pre_act > 0)).astype(jnp.bfloat16)
    act_rows = act_grad.reshape(-1, channels)
    padded = jnp.pad(layer_input, ((0, 0), (1, 1), (1, 1), (0, 0)))
    kernel_grads = []
    input_grad = out_grad
    for offset in range(9):
        row_start = offset // 3
        col_start = offset % 3
        window = padded[:, row_start : row_start + extent, col_start : col_start + extent, :]
        kernel_grads.append(
            lax.dot_general(
                window.reshape(-1, channels),
                act_rows,
                (((0,), (0,)), ((), ())),
                preferred_element_type=jnp.float32,
            )
        )
        if need_input:
            back_term = jnp.dot(act_grad, kernel[offset].T, preferred_element_type=jnp.float32)
            back_padded = jnp.pad(
                back_term, ((0, 0), (row_start, 2 - row_start), (col_start, 2 - col_start), (0, 0))
            )
            input_grad = input_grad + back_padded[:, 1 : 1 + extent, 1 : 1 + extent, :]
    return (jnp.stack(kernel_grads), input_grad)


def torso_backward(layer_inputs, pre_acts, hidden_grad, kernels):
    kernel_grads = [None] * kernels.shape[0]
    out_grad = hidden_grad
    for layer_index in range(kernels.shape[0] - 1, -1, -1):
        kernel_grads[layer_index], out_grad = layer_backward(
            layer_inputs[layer_index],
            pre_acts[layer_index],
            out_grad,
            kernels[layer_index],
            layer_index > 0,
        )
    return jnp.stack(kernel_grads)


def learner_gradient(
    kernels,
    policy_head,
    value_head,
    boards,
    actions,
    behaviour,
    regular,
    rewards,
    trajectory_length,
):
    slot_count = boards.shape[0]
    block_len = math.gcd(slot_count, 16)
    block_count = slot_count // block_len
    board_blocks = boards.reshape((block_count, block_len) + boards.shape[1:])
    action_blocks = actions.reshape(block_count, block_len)
    block_starts = jnp.arange(block_count, dtype=jnp.int32) * block_len
    zero_grad = jnp.zeros(kernels.shape, jnp.float32)

    def first_pass(inputs):
        boards_block, actions_block, block_start = inputs
        hidden, _, _ = torso_forward(boards_block, kernels)
        _, _, policy_log_probs, value_estimates = heads_forward(
            hidden, policy_head, value_head, actions_block
        )
        return (policy_log_probs, value_estimates)

    policy_log_probs, value_estimates = lax.map(
        first_pass, (board_blocks, action_blocks, block_starts)
    )
    policy_gradient_term, value_gradient_term = vee_trace_cotangents(
        policy_log_probs.reshape(-1),
        value_estimates.reshape(-1),
        behaviour,
        regular,
        rewards,
        trajectory_length,
    )
    policy_blocks = policy_gradient_term.reshape(block_count, block_len)
    value_blocks = value_gradient_term.reshape(block_count, block_len)

    def second_pass(running, inputs):
        boards_block, actions_block, policy_block, value_block, block_start = inputs
        hidden, layer_inputs, pre_acts = torso_forward(boards_block, kernels)
        logits, log_total, _, block_values = heads_forward(
            hidden, policy_head, value_head, actions_block
        )
        hidden_grad = heads_backward(
            boards_block.shape,
            policy_block,
            value_block,
            logits,
            log_total,
            block_values,
            actions_block,
            policy_head,
            value_head,
        )
        term = torso_backward(layer_inputs, pre_acts, hidden_grad, kernels)
        return (running + term, None)

    summed_grad, _ = lax.scan(
        second_pass,
        zero_grad,
        (board_blocks, action_blocks, policy_blocks, value_blocks, block_starts),
    )
    return summed_grad.reshape(-1, kernels.shape[-1])


def body(
    board_now,
    traj_boards,
    actions,
    lengths,
    behaviour,
    regular,
    rewards,
    torso,
    policy_head,
    value_head,
    first_moment,
    second_moment,
):
    role_index = lax.axis_index("role")
    dp_index = lax.axis_index("dp")
    channels = torso.shape[1]
    kernels = torso.astype(jnp.bfloat16).reshape(-1, 9, channels, channels)

    def learn():
        return learner_gradient(
            kernels,
            policy_head,
            value_head,
            traj_boards[0],
            actions[0],
            behaviour[0],
            regular[0],
            rewards[0],
            lengths[0],
        )

    def nothing_learned():
        return jnp.zeros(torso.shape, jnp.float32)

    gradient = lax.cond(role_index == 1, learn, nothing_learned)
    share_rows = first_moment.shape[0]
    summed = lax.psum(gradient, "dp")
    square_sum = jnp.sum(summed * summed)
    grad_share = lax.dynamic_slice_in_dim(summed, dp_index * share_rows, share_rows, 0)
    factor = jnp.minimum(1.0, jnp.sqrt(float(gradient.size)) / jnp.sqrt(square_sum + NORM_EPS))
    clipped = grad_share * factor
    moment_one = BETA_ONE * first_moment + (1.0 - BETA_ONE) * clipped
    moment_two = BETA_TWO * second_moment + (1.0 - BETA_TWO) * clipped * clipped
    old_share = lax.dynamic_slice_in_dim(torso, dp_index * share_rows, share_rows, 0)
    weight_share = old_share - LEARN_RATE * moment_one / (jnp.sqrt(moment_two) + ADAM_EPS)
    gathered = lax.all_gather(weight_share, "dp", axis=0, tiled=True)
    new_torso = from_root(gathered, "role", 1)
    new_share = lax.dynamic_slice_in_dim(new_torso, dp_index * share_rows, share_rows, 0)
    new_kernels = new_torso.astype(jnp.bfloat16).reshape(-1, 9, channels, channels)
    hidden, _, _ = torso_forward(board_now, new_kernels)
    logits = policy_logits(hidden, policy_head)
    move_logp = logits - jnp.log(jnp.sum(jnp.exp(logits), axis=1, keepdims=True))
    return (new_share, move_logp)


def solution(mesh):
    return jax.shard_map(
        body,
        mesh=mesh,
        in_specs=(
            P("dp", None, None, None),
            P("dp", None, None, None, None),
            P("dp", None),
            P("dp"),
            P("dp", None),
            P("dp", None),
            P("dp", None),
            P(),
            P(),
            P(),
            P("dp", None),
            P("dp", None),
        ),
        out_specs=(P("dp", None), P("dp", None)),
        check_vma=False,
    )
```

profile of v0, /device:TPU:0, one launch (start us, length us, event | category | flops | bytes accessed | tf_op | source)
XLA Modules:
  0.0 346.9 jit_solution(10073343636483874764)
XLA Ops:
  7.3 1.4 convert_element_type.105
  8.8 0.3 conditional.1
  8.8 0.1 broadcast.93
  9.1 1.0 copy-done.2
  10.1 0.0 all-gather.2.cloned.1.call-start
  10.2 200.6 %all-reduce.15.cloned.1.call-done = f32[2304,128]{1,0:T(8,128)} async-done(((f32[2304,128]{1,0:T(8,128)}), f32[2304,128]{1,0:T(8,128)}) %all-reduce.15.cloned.1.call-update) | async-done | bytes 1179664 | tf_op jit(solution)/shard_map/psum | solution.py:260
  210.7 2.2 multiply_reduce_fusion
  213.6 1.6 fusion.93
  215.3 55.2 %all-gather.2.cloned.1.call-done = f32[2304,128]{1,0:T(8,128)} async-done(((f32[144,128]{1,0:T(8,128)}), f32[2304,128]{1,0:T(8,128)}) %all-gather.2.cloned.1.call-update) | async-done | bytes 1179664 | tf_op jit(solution)/shard_map/all_gather | solution.py:269
  270.5 1.1 broadcast_select_fusion
  271.6 19.9 %all-reduce.17.cloned.1.call-done = f32[2304,128]{1,0:T(8,128)} async-done(((f32[2304,128]{1,0:T(8,128)}), f32[2304,128]{1,0:T(8,128)}) %all-reduce.17.cloned.1.call-update) | async-done | bytes 1179664 | tf_op jit(solution)/shard_map/psum | solution.py:18
  291.6 1.3 convert_element_type.107
  292.9 0.6 fusion.102
  293.5 0.6 fusion.103
  294.1 0.6 fusion.104
  294.6 0.6 fusion.105
  295.2 0.6 fusion.106
  295.8 2.2 fusion.107
  298.0 2.3 fusion.108
  300.3 2.3 fusion.109
  302.6 6.1 %fusion.86 = bf16[64,10,10,128]{3,0,2,1:T(8,128)(2,1)S(1)} fusion(f32[64,10,10,128]{3,0,2,1:T(8,128)S(1)} %fusion.102, f32[64,10,10,128]{3,0,2,1:T(8,128)S(1)} %fusion.103, f32[64,10,10,128]{3,0,2,1:T(8,128)S(1)} %fusion.104, f32[128,64,10,10]{0,1,3,2:T(8,128)S(1)} %fusion.105, f32[64,10,10,128]{3,0,2,1:T(8,128)S(1)} %fusion.106, ...), kind=kOutput, calls=%fused_computation.174 | convolution fusion | flops 179699712 | bytes 31162368 | tf_op jit(solution)/shard_map/dot_general | solution.py:29
  308.7 2.3 fusion.95
  311.0 2.3 fusion.96
  313.3 2.3 fusion.98
  315.6 2.3 fusion.99
  317.8 2.3 fusion.100
  320.1 2.3 fusion.101
  322.5 2.3 fusion.97
  324.8 2.2 fusion.94
  327.0 10.9 %exponential_reduce_fusion = (f32[64]{0:T(128)S(1)}, f32[64,4,10,10]{0,1,3,2:T(4,128)S(1)}) fusion(bf16[128,4]{0,1:T(4,128)(2,1)S(1)} %copy-done.8, f32[64,10,10,128]{3,0,2,1:T(8,128)} %fusion.94, f32[64,10,10,128]{3,0,2,1:T(8,128)} %fusion.95, f32[64,10,10,128]{3,0,2,1:T(8,128)} %fusion.96, f32[64,10,10,128]{3,0,2,1:T(8,128)} %fusion.97, ...), kind=kOutput, calls=%fused_computation.180 | convolution fusion | flops 186278848 | bytes 29627648 | tf_op jit(solution)/shard_map/dot_general | solution.py:46
  338.0 0.8 copy.28
  338.8 1.5 constant_dynamic-slice_fusion
  (32 shorter events, 0.3 us)
Async XLA Ops:
  7.2 1.5 copy-start.8
  7.2 1.5 copy-start.9
  7.2 1.5 copy-start.11
  7.2 1.5 copy-start.12
  7.2 1.5 copy-start.10
  7.2 1.5 copy-start.13
  7.2 1.5 copy-start.1
  7.2 203.5 %all-reduce.15.cloned.1.call-start = ((), (), s32[]{:S(2)}) async-start(), calls=%async_computation | async-start | bytes 2359296 | tf_op jit(solution)/shard_map/psum | solution.py:260
  9.1 1.0 copy-start.2
  9.1 204.5 %copy-start.6 = (f32[144,128]{1,0:T(8,128)S(1)}, f32[144,128]{1,0:T(8,128)}, u32[]{:S(2)}) copy-start(f32[144,128]{1,0:T(8,128)} %param.27) | copy-start | bytes 221188
  9.1 204.5 %copy-start.7 = (f32[144,128]{1,0:T(8,128)S(1)}, f32[144,128]{1,0:T(8,128)}, u32[]{:S(2)}) copy-start(f32[144,128]{1,0:T(8,128)} %param.26) | copy-start | bytes 221188
  10.1 260.4 %all-gather.2.cloned.1.call-start = ((), (), s32[]{:S(2)}) async-start(), calls=%async_computation.1 | async-start | bytes 1253376 | tf_op jit(solution)/shard_map/all_gather | solution.py:269
  215.3 76.3 %all-reduce.17.cloned.1.call-start = ((), (), s32[]{:S(2)}) async-start(), calls=%async_computation.2 | async-start | bytes 2359296 | tf_op jit(solution)/shard_map/psum | solution.py:18
  271.6 21.3 %copy-start = (bf16[64,10,10,128]{3,0,2,1:T(8,128)(2,1)S(1)}, bf16[64,10,10,128]{3,0,2,1:T(8,128)(2,1)}, u32[]{:S(2)}) copy-start(bf16[64,10,10,128]{3,0,2,1:T(8,128)(2,1)} %param.16) | copy-start | bytes 4915204
  292.9 31.8 %copy-start.3 = (bf16[2304,128]{1,0:T(8,128)(2,1)}, bf16[2304,128]{1,0:T(8,128)(2,1)S(1)}, u32[]{:S(2)}) copy-start(bf16[2304,128]{1,0:T(8,128)(2,1)S(1)} %convert_element_type.107) | copy-start | bytes 1769476
Sparse Core Ops, SparseCore 0:
  13.6 197.1 all-reduce.14
  215.4 55.0 all-gather.1
  272.8 18.6 all-reduce.16
where the time goes:
time: 348 us; the launch traced here: 347 us
  waiting for transfers between devices  276 us (79%)
  matrix products  45 us (13%)
  between operations  14.7 us (4%)
  other arithmetic  7.65 us (2%)
    psum x1, waiting for transfers between devices, body(): summed = lax.psum(gradient, 'dp')  201 us
    all_gather x1, waiting for transfers between devices, body(): gathered = lax.all_gather(weight_share, 'dp', axis=0, tiled=True)  55.2 us
    dot_general x17, matrix products, conv_sum(): jnp.dot(window, kernel[offset], preferred_element_type=jnp.float32)  34 us
    psum x1, waiting for transfers between devices, from_root(): return lax.psum(jnp.where(mine, x, jnp.zeros_like(x)), axis)  19.9 us
    dot_general x1, matrix products, policy_logits(): per_cell = jnp.dot(hidden, policy_head, preferred_element_type=jnp.float32)  10.9 us
  transfers between devices with their start and end apart: 3, of which 3 were waited for; matrix products, arithmetic and copies ran while one was open for 0% of the time, Pallas kernels for 0%

commit v1 on v0

v1 whole, which is shorter than its diff:
```python
import functools

import jax
import jax.numpy as jnp
from jax import lax
from jax.experimental import pallas as pl
from jax.experimental.pallas import tpu as pltpu
from jax.sharding import PartitionSpec as P

ETA = 0.2
LEARN_RATE = 0.03
BETA_ONE = 0.9
BETA_TWO = 0.999
ADAM_EPS = 1e-08
NORM_EPS = 1e-12
SIDE = 10
CELLS = 100
CH = 128
TAPS = 9 * CH
F32 = jnp.float32
BF16 = jnp.bfloat16
MESH = pl.DeviceIdType.MESH


def vmem():
    return pl.BlockSpec(memory_space=pltpu.VMEM)


def fill_padded(boards, flat, padded, games):
    padded[...] = jnp.zeros(padded.shape, padded.dtype)

    def widen(step, carry):
        for part in range(10):
            at = step * 10 + part
            flat[pl.ds(pl.multiple_of(at * 16, 16), SIDE), :] = boards[at].astype(F32)
        return carry

    lax.fori_loop(0, games, widen, 0)

    def place(i, carry):
        for j in range(SIDE):
            rows = flat[pl.ds(i * 16 + j, games, stride=160), :]
            padded[i + 1, j + 1] = rows.astype(BF16)
        return carry

    lax.fori_loop(0, SIDE, place, 0)


def columns(padded, i, rows, games, flip):
    parts = []
    for p in range(3):
        for q in range(3):
            u, v = (2 - p, 2 - q) if flip else (p, q)
            window = padded[pl.ds(i + u, rows), v : v + SIDE]
            parts.append(window.reshape(rows * SIDE * games, CH))
    return jnp.concatenate(parts, axis=1)


def inner(padded, i, rows, games):
    return padded[pl.ds(i + 1, rows), 1 : 1 + SIDE].reshape(rows * SIDE * games, CH)


def lane_sum(x, games):
    shift = 64
    while shift >= games:
        x = x + pltpu.roll(x, shift, 1)
        shift //= 2
    return x


def spread_heads(head_ref, games, amount):
    rows = [jnp.broadcast_to(head_ref[d : d + 1, :], (games, CH)) for d in range(amount)]
    if games * amount < CH:
        rows.append(jnp.zeros((CH - games * amount, CH), F32))
    return jnp.concatenate(rows, axis=0).astype(BF16)


def own_lane(games):
    game = lax.broadcasted_iota(jnp.int32, (games, CH), 0)
    lane = lax.broadcasted_iota(jnp.int32, (games, CH), 1)
    return (lane % games == game).astype(F32)


def learner_kernel(
    boards,
    actions,
    lengths,
    behaviour,
    regular,
    rewards,
    torso,
    head,
    grad,
    flat,
    h0,
    h1,
    a1,
    a0,
    weights,
    turned,
    pre,
    hidden_grad,
    cells,
    small,
    heads,
    total,
):
    games, rows = 16, 2
    block = rows * SIDE * games
    role = lax.axis_index("role")
    weights[...] = torso[...].astype(BF16)
    fill_padded(boards, flat, h0, games)
    h1[...] = jnp.zeros(h1.shape, BF16)
    a1[...] = jnp.zeros(a1.shape, BF16)
    heads[...] = spread_heads(head, games, 5)
    mine = own_lane(games)

    def layer_one(step, carry):
        i = step * rows
        act = jnp.dot(columns(h0, i, rows, games, False), weights[0:TAPS], preferred_element_type=F32)
        pre[0, pl.ds(pl.multiple_of(step * block, block), block)] = act
        h = (inner(h0, i, rows, games).astype(F32) + jnp.maximum(act, 0.0)).astype(BF16)
        h1[pl.ds(i + 1, rows), 1 : 1 + SIDE] = h.reshape(rows, SIDE, games, CH)
        return carry

    lax.fori_loop(0, SIDE // rows, layer_one, 0)

    def layer_two(step, carry):
        i = step * rows
        act = jnp.dot(
            columns(h1, i, rows, games, False), weights[TAPS : 2 * TAPS], preferred_element_type=F32
        )
        pre[1, pl.ds(pl.multiple_of(step * block, block), block)] = act
        h = (inner(h1, i, rows, games).astype(F32) + jnp.maximum(act, 0.0)).astype(BF16)
        out = lax.dot_general(h, heads[...], (((1,), (1,)), ((), ())), preferred_element_type=F32)
        picked = jnp.sum(out.reshape(rows * SIDE, games, CH) * mine[None], axis=1)
        cells[pl.ds(i, rows)] = picked.reshape(rows, SIDE, CH)
        return carry

    lax.fori_loop(0, SIDE // rows, layer_two, 0)

    small[...] = jnp.zeros(small.shape, F32)
    small[0:1, 0:games] = actions[...].astype(F32)
    small[1:2, 0:games] = behaviour[...]
    small[2:3, 0:games] = regular[...]
    small[3:4, 0:games] = rewards[...]
    given = lane_sum(small[...], games)
    action = given[0:1].astype(jnp.int32)
    behave, regul, reward = given[1:2], given[2:3], given[3:4]

    lane = lax.broadcasted_iota(jnp.int32, (1, CH), 1)
    slot = lane % games
    policy_lane = lane < 4 * games
    logits = cells[...]
    cell_id = lax.broadcasted_iota(jnp.int32, logits.shape, 0) * SIDE + lax.broadcasted_iota(
        jnp.int32, logits.shape, 1
    )
    lane_full = lax.broadcasted_iota(jnp.int32, logits.shape, 2)
    taken = (lane_full // games) * CELLS + cell_id == action.reshape(1, 1, CH)
    policy_full = lane_full < 4 * games
    taken = jnp.where(policy_full, jnp.where(taken, 1.0, 0.0), 0.0)
    logits = jnp.where(policy_full, logits, 0.0)

    def over_cells(x):
        return jnp.sum(jnp.sum(x, axis=0), axis=0, keepdims=True)

    exps = jnp.where(policy_full, jnp.exp(logits), 0.0)
    log_total = jnp.log(lane_sum(over_cells(exps), games))
    logp = lane_sum(over_cells(taken * logits), games) - log_total
    value_lane = jnp.where((lane >= 4 * games) & (lane < 5 * games), 1.0, 0.0)
    values = jnp.tanh(lane_sum(over_cells(cells[...]) * value_lane, games) / CELLS)

    def ahead(x, by):
        return jnp.where(slot + by < games, pltpu.roll(x, CH - by, 1), 0.0)

    length = lengths[0]
    live = jnp.where(slot < length, 1.0, 0.0)
    next_live = jnp.where(slot + 1 < length, 1.0, 0.0)
    ratio = jnp.minimum(1.0, jnp.exp(logp - behave))
    shaped = reward - ETA * (logp - regul)
    delta = live * ratio * (shaped + ahead(values, 1) * next_live - values)
    correction, slope = live * delta, live * ratio
    by = 1
    while by < games:
        correction = correction + slope * ahead(correction, by)
        slope = slope * ahead(slope, by)
        by *= 2
    targets = values + correction
    policy_term = -live * ratio * (shaped + ahead(targets, 1) * next_live - values)
    value_term = -live * (targets - values)
    value_cell = value_term * (1.0 - values * values) / CELLS * value_lane

    probs = jnp.exp(logits - log_total.reshape(1, 1, CH))
    cells[...] = jnp.where(
        policy_full,
        policy_term.reshape(1, 1, CH) * (taken - probs),
        jnp.broadcast_to(value_cell.reshape(1, 1, CH), logits.shape),
    )

    def top(step, carry):
        i = step * rows
        at = pl.ds(pl.multiple_of(step * block, block), block)
        g = cells[pl.ds(i, rows)].reshape(rows * SIDE, 1, CH) * mine[None]
        g = g.reshape(block, CH)
        high = g.astype(BF16)
        low = (g - high.astype(F32)).astype(BF16)
        out = jnp.dot(high, heads[...], preferred_element_type=F32)
        out = out + jnp.dot(low, heads[...], preferred_element_type=F32)
        hidden_grad[at] = out
        act = jnp.where(pre[1, at] > 0, out, 0.0).astype(BF16)
        a1[pl.ds(i + 1, rows), 1 : 1 + SIDE] = act.reshape(rows, SIDE, games, CH)
        return carry

    lax.fori_loop(0, SIDE // rows, top, 0)

    def weight_grad(h, a):
        total[...] = jnp.zeros(total.shape, F32)

        def add(step, carry):
            i = step * rows
            total[...] += lax.dot_general(
                inner(h, i, rows, games),
                columns(a, i, rows, games, True),
                (((0,), (0,)), ((), ())),
                preferred_element_type=F32,
            )
            return carry

        lax.fori_loop(0, SIDE // rows, add, 0)
        for offset in range(9):
            grad[offset * CH : (offset + 1) * CH, :] = total[:, offset * CH : (offset + 1) * CH]

    @pl.when(role == 1)
    def _():
        weight_grad(h1, a1)

    @pl.when(role == 0)
    def _():
        a0[...] = jnp.zeros(a0.shape, BF16)
        for offset in range(9):
            at = TAPS + offset * CH
            turned[offset * CH : (offset + 1) * CH, :] = weights[at : at + CH, :].astype(F32).T.astype(BF16)

        def back(step, carry):
            i = step * rows
            at = pl.ds(pl.multiple_of(step * block, block), block)
            out = hidden_grad[at] + jnp.dot(
                columns(a1, i, rows, games, True), turned[...], preferred_element_type=F32
            )
            act = jnp.where(pre[0, at] > 0, out, 0.0).astype(BF16)
            a0[pl.ds(i + 1, rows), 1 : 1 + SIDE] = act.reshape(rows, SIDE, games, CH)
            return carry

        lax.fori_loop(0, SIDE // rows, back, 0)
        weight_grad(h0, a0)


def learner(boards, actions, lengths, behaviour, regular, rewards, torso, head):
    padded = (SIDE + 2, SIDE + 2, 16, CH)
    in_specs = [vmem() for _ in range(8)]
    in_specs[2] = pl.BlockSpec(memory_space=pltpu.SMEM)
    return pl.pallas_call(
        learner_kernel,
        out_shape=jax.ShapeDtypeStruct((TAPS, CH), F32),
        in_specs=in_specs,
        out_specs=vmem(),
        scratch_shapes=[
            pltpu.VMEM((16 * 160, CH), F32),
            pltpu.VMEM(padded, BF16),
            pltpu.VMEM(padded, BF16),
            pltpu.VMEM(padded, BF16),
            pltpu.VMEM(padded, BF16),
            pltpu.VMEM((2 * TAPS, CH), BF16),
            pltpu.VMEM((TAPS, CH), BF16),
            pltpu.VMEM((2, 1600, CH), F32),
            pltpu.VMEM((1600, CH), F32),
            pltpu.VMEM((SIDE, SIDE, CH), F32),
            pltpu.VMEM((8, CH), F32),
            pltpu.VMEM((CH, CH), BF16),
            pltpu.VMEM((CH, TAPS), F32),
        ],
        compiler_params=pltpu.CompilerParams(vmem_limit_bytes=48 << 20),
    )(boards, actions, lengths, behaviour, regular, rewards, torso, head)


def update_kernel(
    grad,
    torso,
    moment_one,
    moment_two,
    out,
    plane,
    quarter,
    line,
    norms,
    s1,
    r1,
    s2,
    r2,
    sn,
    rn,
    sz,
    rz,
    sp,
    rp,
    ss,
    rs,
):
    share = moment_one.shape[0]
    role = lax.axis_index("role")
    dp = lax.axis_index("dp")
    z, spot = dp // 4, dp % 4
    owner = z // 2 == role

    def send(src, dst, send_sem, recv_sem, to_role, to_dp):
        copy = pltpu.make_async_remote_copy(
            src_ref=src,
            dst_ref=dst,
            send_sem=send_sem,
            recv_sem=recv_sem,
            device_id=(to_role, to_dp),
            device_id_type=MESH,
        )
        return copy

    barrier = pltpu.get_barrier_semaphore()

    def greet(to_role, to_dp):
        pl.semaphore_signal(barrier, inc=1, device_id=(to_role, to_dp), device_id_type=MESH)

    @pl.when(owner)
    def _():
        for k in range(1, 16):
            other = (dp + k) % 16
            greet(other // 8, other)
        for o in range(2):
            greet(role, (2 - 2 * role + o) * 4 + spot)
        greet(1 - role, dp)
        pl.semaphore_wait(barrier, 18)

    @pl.when(jnp.logical_not(owner))
    def _():
        for k in range(1, 4):
            greet(role, z * 4 + (spot + k) % 4)
            greet(role, ((z + k) % 4) * 4 + spot)
        greet(1 - role, dp)
        pl.semaphore_wait(barrier, 7)

    def rows(index):
        return pl.ds(pl.multiple_of(index * share, 8), share)

    def to_plane(o, k):
        p = (spot + k) % 4
        return send(
            grad.at[rows(4 * o + p)],
            plane.at[o, spot],
            s1.at[o, k - 1],
            r1.at[o, spot],
            role,
            z * 4 + p,
        )

    def from_plane(o, k):
        p = (spot + k) % 4
        return send(
            grad.at[rows(4 * o + p)], plane.at[o, p], s1.at[o, k - 1], r1.at[o, p], role, z * 4 + p
        )

    for o in range(2):
        for k in range(1, 4):
            to_plane(o, k).start()

    def to_owner(o):
        return send(
            quarter.at[o], line.at[z], s2.at[o], r2.at[z], role, (2 * role + o) * 4 + spot
        )

    for o in range(2):
        summed = grad[rows(4 * o + spot)]
        for k in range(1, 4):
            from_plane(o, k).wait_recv()
            summed = summed + plane[o, (spot + k) % 4]
        quarter[o] = summed

        @pl.when(z != 2 * role + o)
        def _():
            to_owner(o).start()

    def to_norm(k):
        other = (dp + k) % 16
        return send(norms.at[dp], norms.at[dp], sn.at[k - 1], rn.at[dp], other // 8, other)

    def from_norm(k):
        other = (dp + k) % 16
        return send(norms.at[other], norms.at[other], sn.at[k - 1], rn.at[other], other // 8, other)

    def share_ref(to, index):
        return out.at[rows(index)]

    def down_line(k):
        return send(
            out.at[rows(dp)],
            out.at[rows(dp)],
            sz.at[k - 1],
            rz.at[z % 2],
            role,
            ((z + k) % 4) * 4 + spot,
        )

    @pl.when(owner)
    def _():
        summed = quarter[z % 2]
        for k in range(1, 4):
            other = (z + k) % 4
            send(
                quarter.at[0], line.at[other], s2.at[0], r2.at[other], role, other * 4 + spot
            ).wait_recv()
            summed = summed + line[other]
        norms[dp] = jnp.sum((summed * summed).reshape(share // 8, 8, CH), axis=0)
        for k in range(1, 16):
            to_norm(k).start()
        for k in range(1, 16):
            from_norm(k).wait_recv()
        square_sum = jnp.sum(jnp.sum(norms[...], axis=0), axis=0, keepdims=True)
        square_sum = jnp.sum(square_sum, axis=1, keepdims=True)
        size = float(torso.shape[0] * torso.shape[1])
        factor = jnp.minimum(1.0, jnp.sqrt(jnp.full((1, 1), size, F32)) / jnp.sqrt(square_sum + NORM_EPS))
        clipped = summed * factor
        one = BETA_ONE * moment_one[...] + (1.0 - BETA_ONE) * clipped
        two = BETA_TWO * moment_two[...] + (1.0 - BETA_TWO) * clipped * clipped
        out[rows(dp)] = torso[rows(dp)] - LEARN_RATE * one / (jnp.sqrt(two) + ADAM_EPS)
        for k in range(1, 4):
            down_line(k).start()

    def to_peer(o, k):
        p = (spot + k) % 4
        at = out.at[rows((2 * role + o) * 4 + spot)]
        return send(at, at, sp.at[o, k - 1], rp.at[o, spot], role, z * 4 + p)

    def to_sibling(o, k):
        p = (spot + k) % 4
        at = out.at[rows((2 * role + o) * 4 + p)]
        return send(at, at, ss.at[o, k], rs.at[o, p], 1 - role, dp)

    for o in range(2):
        at = out.at[rows((2 * role + o) * 4 + spot)]

        @pl.when(z != 2 * role + o)
        def _():
            send(at, at, sz.at[0], rz.at[o], role, (2 * role + o) * 4 + spot).wait_recv()

        for k in range(1, 4):
            to_peer(o, k).start()
        to_sibling(o, 0).start()
    for o in range(2):
        for k in range(1, 4):
            p = (spot + k) % 4
            at = out.at[rows((2 * role + o) * 4 + p)]
            send(at, at, sp.at[o, k - 1], rp.at[o, p], role, z * 4 + p).wait_recv()
            to_sibling(o, k).start()
    for o in range(2):
        for p in range(4):
            at = out.at[rows((2 - 2 * role + o) * 4 + p)]
            send(at, at, ss.at[o, p], rs.at[o, p], 1 - role, dp).wait_recv()
    for o in range(2):
        for k in range(1, 4):
            to_plane(o, k).wait_send()
            to_peer(o, k).wait_send()
        for k in range(4):
            to_sibling(o, k).wait_send()

        @pl.when(z != 2 * role + o)
        def _():
            to_owner(o).wait_send()

    @pl.when(owner)
    def _():
        for k in range(1, 16):
            to_norm(k).wait_send()
        for k in range(1, 4):
            down_line(k).wait_send()


def update_any(grad, torso, moment_one, moment_two):
    share = moment_one.shape[0]
    summed = lax.all_gather(lax.psum(grad, "dp"), "role", axis=0, tiled=True)
    start = lax.axis_index("dp") * share
    square_sum = jnp.sum(summed * summed)
    factor = jnp.minimum(1.0, jnp.sqrt(float(summed.size)) / jnp.sqrt(square_sum + NORM_EPS))
    clipped = lax.dynamic_slice_in_dim(summed, start, share, 0) * factor
    one = BETA_ONE * moment_one + (1.0 - BETA_ONE) * clipped
    two = BETA_TWO * moment_two + (1.0 - BETA_TWO) * clipped * clipped
    old = lax.dynamic_slice_in_dim(torso, start, share, 0)
    new = old - LEARN_RATE * one / (jnp.sqrt(two) + ADAM_EPS)
    return lax.all_gather(new, "dp", axis=0, tiled=True)


def update(grad, torso, moment_one, moment_two):
    share = moment_one.shape[0]
    if lax.axis_size("dp") != 16 or lax.axis_size("role") != 2:
        return update_any(grad, torso, moment_one, moment_two)
    dma = pltpu.SemaphoreType.DMA
    return pl.pallas_call(
        update_kernel,
        out_shape=jax.ShapeDtypeStruct(torso.shape, F32),
        in_specs=[vmem() for _ in range(4)],
        out_specs=vmem(),
        scratch_shapes=[
            pltpu.VMEM((2, 4, share, CH), F32),
            pltpu.VMEM((2, share, CH), F32),
            pltpu.VMEM((4, share, CH), F32),
            pltpu.VMEM((16, 8, CH), F32),
            dma((2, 3)),
            dma((2, 4)),
            dma((2,)),
            dma((4,)),
            dma((15,)),
            dma((16,)),
            dma((3,)),
            dma((2,)),
            dma((2, 3)),
            dma((2, 4)),
            dma((2, 4)),
            dma((2, 4)),
        ],
        compiler_params=pltpu.CompilerParams(
            collective_id=0, has_side_effects=True, vmem_limit_bytes=32 << 20
        ),
    )(grad, torso, moment_one, moment_two)


def actor_kernel(games, boards, torso, head, out, raw, flat, h0, h1, weights, cells, heads, sem):
    rows = 1
    block = rows * SIDE * games
    role = lax.axis_index("role")
    start = pl.multiple_of(role * games * SIDE, 8)
    copy = pltpu.make_async_copy(boards.at[pl.ds(start, games * SIDE)], raw, sem)
    copy.start()
    weights[...] = torso[...].astype(BF16)
    h1[...] = jnp.zeros(h1.shape, BF16)
    heads[...] = spread_heads(head, games, 4)
    cells[...] = jnp.zeros(cells.shape, F32)
    copy.wait()
    fill_padded(raw, flat, h0, games)
    mine = own_lane(games)

    def layer_one(step, carry):
        i = step * rows
        act = jnp.dot(columns(h0, i, rows, games, False), weights[0:TAPS], preferred_element_type=F32)
        h = (inner(h0, i, rows, games).astype(F32) + jnp.maximum(act, 0.0)).astype(BF16)
        h1[pl.ds(i + 1, rows), 1 : 1 + SIDE] = h.reshape(rows, SIDE, games, CH)
        return carry

    lax.fori_loop(0, SIDE // rows, layer_one, 0)

    def layer_two(step, carry):
        i = step * rows
        act = jnp.dot(
            columns(h1, i, rows, games, False), weights[TAPS : 2 * TAPS], preferred_element_type=F32
        )
        h = (inner(h1, i, rows, games).astype(F32) + jnp.maximum(act, 0.0)).astype(BF16)
        res = lax.dot_general(h, heads[...], (((1,), (1,)), ((), ())), preferred_element_type=F32)
        picked = jnp.sum(res.reshape(rows * SIDE, games, CH) * mine[None], axis=1)
        cells[pl.ds(step * SIDE, SIDE), :] = picked
        return carry

    lax.fori_loop(0, SIDE // rows, layer_two, 0)
    logits = cells[...]
    cell_id = lax.broadcasted_iota(jnp.int32, logits.shape, 0)
    exps = jnp.where(cell_id < CELLS, jnp.exp(logits), 0.0)
    log_total = jnp.log(lane_sum(jnp.sum(exps, axis=0, keepdims=True), games))
    turned = (logits - log_total).T
    for d in range(4):
        out[:, d * CELLS : (d + 1) * CELLS] = turned[d * games : (d + 1) * games, 0:CELLS]


def actor(boards, torso, head, games):
    padded = (SIDE + 2, SIDE + 2, games, CH)
    return pl.pallas_call(
        functools.partial(actor_kernel, games),
        out_shape=jax.ShapeDtypeStruct((games, 4 * CELLS), F32),
        in_specs=[pl.BlockSpec(memory_space=pl.ANY), vmem(), vmem()],
        out_specs=vmem(),
        scratch_shapes=[
            pltpu.VMEM((games * SIDE, SIDE, CH), BF16),
            pltpu.VMEM((games * 160, CH), F32),
            pltpu.VMEM(padded, BF16),
            pltpu.VMEM(padded, BF16),
            pltpu.VMEM((2 * TAPS, CH), BF16),
            pltpu.VMEM((CH, CH), F32),
            pltpu.VMEM((CH, CH), BF16),
            pltpu.SemaphoreType.DMA,
        ],
        compiler_params=pltpu.CompilerParams(vmem_limit_bytes=48 << 20),
    )(boards, torso, head)


def join_kernel(part, out, send_sem, recv_sem):
    games = part.shape[0]
    role = lax.axis_index("role")
    dp = lax.axis_index("dp")
    barrier = pltpu.get_barrier_semaphore()
    pl.semaphore_signal(barrier, inc=1, device_id=(1 - role, dp), device_id_type=MESH)
    pl.semaphore_wait(barrier, 1)
    mine = pl.ds(pl.multiple_of(role * games, 8), games)
    copy = pltpu.make_async_remote_copy(
        src_ref=part,
        dst_ref=out.at[mine],
        send_sem=send_sem,
        recv_sem=recv_sem,
        device_id=(1 - role, dp),
        device_id_type=MESH,
    )
    copy.start()
    out[mine] = part[...]
    copy.wait()


def join(part):
    return pl.pallas_call(
        join_kernel,
        out_shape=jax.ShapeDtypeStruct((2 * part.shape[0], part.shape[1]), F32),
        in_specs=[vmem()],
        out_specs=vmem(),
        scratch_shapes=[pltpu.SemaphoreType.DMA, pltpu.SemaphoreType.DMA],
        compiler_params=pltpu.CompilerParams(collective_id=1, has_side_effects=True),
    )(part)


def body(
    board_now,
    traj_boards,
    actions,
    lengths,
    behaviour,
    regular,
    rewards,
    torso,
    policy_head,
    value_head,
    first_moment,
    second_moment,
):
    dp_index = lax.axis_index("dp")
    head = jnp.concatenate(
        [policy_head.T, value_head[None, :], jnp.zeros((3, CH), BF16)], axis=0
    ).astype(F32)
    boards = traj_boards.reshape(-1, SIDE, CH)
    grad = learner(boards, actions, lengths, behaviour, regular, rewards, torso, head)
    weights = update(grad, torso, first_moment, second_moment)
    share_rows = first_moment.shape[0]
    new_share = lax.dynamic_slice_in_dim(weights, dp_index * share_rows, share_rows, 0)
    games = board_now.shape[0] // 2
    part = actor(board_now.reshape(-1, SIDE, CH), weights, head, games)
    return (new_share, join(part))


def solution(mesh):
    return jax.shard_map(
        body,
        mesh=mesh,
        in_specs=(
            P("dp", None, None, None),
            P("dp", None, None, None, None),
            P("dp", None),
            P("dp"),
            P("dp", None),
            P("dp", None),
            P("dp", None),
            P(),
            P(),
            P(),
            P("dp", None),
            P("dp", None),
        ),
        out_specs=(P("dp", None), P("dp", None)),
        check_vma=False,
    )
```

time: 348 us -> 70.3 us (0.20)
  the two profiles are of different devices: /device:TPU:0 before, /device:TPU:9 now
where the time goes in v1:
time: 70.3 us; the launch traced here: 70 us
  Pallas kernels  58.7 us (83%)
  local copies, waits for them, and re-layouts  9.15 us (13%)
  between operations  1.37 us (2%)
  other arithmetic  0.77 us (1%)
    pallas_call x1, Pallas kernels, update(): pl.pallas_call(update_kernel, out_shape=jax.ShapeDtypeStruct(torso.shape,...  36.1 us
    pallas_call x1, Pallas kernels, actor(): pl.pallas_call(functools.partial(actor_kernel, games), out_shape=jax.Shap...  10.9 us
    pallas_call x1, Pallas kernels, learner(): pl.pallas_call(learner_kernel, out_shape=jax.ShapeDtypeStruct((TAPS, CH),...  8.95 us
    unnamed x21, local copies, waits for them, and re-layouts  8.42 us
    pallas_call x1, Pallas kernels, join(): pl.pallas_call(join_kernel, out_shape=jax.ShapeDtypeStruct((2 * part.shap...  2.76 us

profile of v1, /device:TPU:9, one launch (start us, length us, event | category | flops | bytes accessed | tf_op | source)
XLA Modules:
  0.0 70.0 jit_solution(14370760476485967922)
XLA Ops:
  1.3 0.1 pad.2.clone
  1.4 0.8 %maximum_convert_fusion.head = f32[8,128]{1,0:T(8,128)S(1)} fusion(bf16[1,128]{1,0:T(2,128)(2,1)} %bitcast.7, bf16[4,128]{1,0:T(4,128)(2,1)} %bitcast.6, bf16[8]{0:T(256)(128)(2,1)S(1)} %pad.2.clone), kind=kLoop, calls=%fused_computation | loop fusion | flops 6144 | bytes 5392 | tf_op jit(solution)/shard_map/convert_element_type | solution.py:647
  2.1 1.1 %copy.14 = bf16[1,16,10,10,128]{4,3,2,1,0:T(8,128)(2,1)S(1)} copy(bf16[1,16,10,10,128]{4,1,3,2,0:T(8,128)(2,1)} %param.13) | data formatting | bytes 819200 | tf_op args[1]
  3.3 0.0 copy-start
  3.3 1.3 %copy-done = f32[2304,128]{1,0:T(8,128)S(1)} copy-done((f32[2304,128]{1,0:T(8,128)S(1)}, f32[2304,128]{1,0:T(8,128)}, u32[]{:S(2)}) %copy-start) | copy-done | bytes 1179672
  4.6 0.0 copy-start.4
  4.6 0.7 copy-done.4
  5.2 0.0 copy-start.5
  5.2 0.7 copy-done.5
  5.9 0.0 copy-start.6
  5.9 0.7 copy-done.6
  6.5 0.0 copy-start.7
  6.5 0.7 copy-done.7
  7.2 0.0 copy-start.2
  7.2 0.0 copy-start.3
  7.2 8.9 %shard_map.131.grad = f32[1152,128]{1,0:T(8,128)S(1)} custom-call(bf16[160,10,128]{2,1,0:T(8,128)(2,1)S(1)} %bitcast.5, s32[1,16]{1,0:T(1,128)S(1)} %copy-done.4, s32[1]{0:T(128)S(6)} %copy.17.lengths, f32[1,16]{1,0:T(1,128)S(1)} %copy-done.5, f32[1,16]{1,0:T(1,128)S(1)} %copy-done.6, f32[1,16]{1,0:T(1,128)S(1)} %copy-done.7, f32[2304,128]{1,0:T(8,128)S(1)} %copy-done, ...), custom_call_target="tpu_custom_call" | custom-call | tf_op jit(solution)/shard_map/pallas_call | solution.py:262
  16.1 0.0 copy-done.2
  16.1 0.0 copy-done.3
  16.2 0.0 copy-start.8
  16.2 36.1 %shard_map.132.torso = f32[2304,128]{1,0:T(8,128)S(1)} custom-call(f32[1152,128]{1,0:T(8,128)S(1)} %shard_map.131.grad, f32[2304,128]{1,0:T(8,128)S(1)} %copy-done, f32[144,128]{1,0:T(8,128)S(1)} %copy-done.2, f32[144,128]{1,0:T(8,128)S(1)} %copy-done.3), custom_call_target="tpu_custom_call" | custom-call | tf_op jit(solution)/shard_map/pallas_call | solution.py:503
  52.3 0.6 constant_dynamic-slice_fusion
  53.0 0.0 copy-done.8
  53.0 1.2 %copy.15 = bf16[64,10,10,128]{3,2,1,0:T(8,128)(2,1)S(1)} copy(bf16[64,10,10,128]{3,0,2,1:T(8,128)(2,1)S(1)} %copy-done.8) | data formatting | bytes 3276800 | tf_op args[0]
  54.2 10.9 %shard_map.133.part = f32[32,400]{1,0:T(8,128)S(1)} custom-call(bf16[640,10,128]{2,1,0:T(8,128)(2,1)S(1)} %bitcast.4, f32[2304,128]{1,0:T(8,128)S(1)} %shard_map.132.torso, f32[8,128]{1,0:T(8,128)S(1)} %maximum_convert_fusion.head), custom_call_target="tpu_custom_call" | custom-call | tf_op jit(solution)/shard_map/pallas_call | solution.py:579
  65.0 0.0 copy-start.1
  65.1 0.6 copy-done.1
  65.7 2.8 %shard_map.134 = f32[64,400]{1,0:T(8,128)} custom-call(f32[32,400]{1,0:T(8,128)} %copy-done.1), custom_call_target="tpu_custom_call" | custom-call | tf_op jit(solution)/shard_map/pallas_call | solution.py:620
  68.4 1.6 %copy.18 = f32[64,400]{1,0:T(8,128)} copy(f32[64,400]{1,0:T(8,128)} %shard_map.134) | data formatting | bytes 204800
  (1 shorter events, 0.0 us)
Async XLA Ops:
  3.3 1.3 %copy-start = (f32[2304,128]{1,0:T(8,128)S(1)}, f32[2304,128]{1,0:T(8,128)}, u32[]{:S(2)}) copy-start(f32[2304,128]{1,0:T(8,128)} %torso.3) | copy-start | bytes 3538948
  4.6 0.7 copy-start.4
  5.2 0.7 copy-start.5
  5.9 0.7 copy-start.6
  6.5 0.7 copy-start.7
  7.2 9.0 %copy-start.2 = (f32[144,128]{1,0:T(8,128)S(1)}, f32[144,128]{1,0:T(8,128)}, u32[]{:S(2)}) copy-start(f32[144,128]{1,0:T(8,128)} %moment_one.1) | copy-start | bytes 221188
  7.2 9.0 %copy-start.3 = (f32[144,128]{1,0:T(8,128)S(1)}, f32[144,128]{1,0:T(8,128)}, u32[]{:S(2)}) copy-start(f32[144,128]{1,0:T(8,128)} %moment_two.1) | copy-start | bytes 221188
  16.2 36.8 %copy-start.8 = (bf16[64,10,10,128]{3,0,2,1:T(8,128)(2,1)S(1)}, bf16[64,10,10,128]{3,0,2,1:T(8,128)(2,1)}, u32[]{:S(2)}) copy-start(bf16[64,10,10,128]{3,0,2,1:T(8,128)(2,1)} %param.12) | copy-start | bytes 4915204
  65.0 0.6 copy-start.1

commit v2 on v1

v2 whole, which is shorter than its diff:
```python
import functools

import jax
import jax.numpy as jnp
from jax import lax
from jax.experimental import pallas as pl
from jax.experimental.pallas import tpu as pltpu
from jax.sharding import PartitionSpec as P

ETA = 0.2
LEARN_RATE = 0.03
BETA_ONE = 0.9
BETA_TWO = 0.999
ADAM_EPS = 1e-08
NORM_EPS = 1e-12
SIDE = 10
CELLS = 100
CH = 128
TAPS = 9 * CH
ROWS = 5
F32 = jnp.float32
BF16 = jnp.bfloat16
MESH = pl.DeviceIdType.MESH


def vmem():
    return pl.BlockSpec(memory_space=pltpu.VMEM)


def columns(padded, i, games, flip, first=0, last=9):
    parts = []
    for offset in range(first, last):
        p, q = offset // 3, offset % 3
        u, v = (2 - p, 2 - q) if flip else (p, q)
        window = padded[pl.ds(i + u, ROWS), v : v + SIDE]
        parts.append(window.reshape(ROWS * SIDE * games, CH))
    return jnp.concatenate(parts, axis=1)


def inner(padded, i, games):
    return padded[pl.ds(i + 1, ROWS), 1 : 1 + SIDE].reshape(ROWS * SIDE * games, CH)


def set_inner(padded, i, games, value):
    padded[pl.ds(i + 1, ROWS), 1 : 1 + SIDE] = value.reshape(ROWS, SIDE, games, CH)


def clear_rim(padded):
    zero = jnp.zeros((1, SIDE + 2) + padded.shape[2:], padded.dtype)
    side = jnp.zeros((SIDE, 1) + padded.shape[2:], padded.dtype)
    padded[0:1] = zero
    padded[SIDE + 1 : SIDE + 2] = zero
    padded[1 : SIDE + 1, 0:1] = side
    padded[1 : SIDE + 1, SIDE + 1 : SIDE + 2] = side


def center(padded):
    return padded.at[pl.ds(1, SIDE), pl.ds(1, SIDE)]


def steps(f):
    def one(step, carry):
        f(step, step * ROWS)
        return carry

    lax.fori_loop(0, SIDE // ROWS, one, 0)


def lane_sum(x, games):
    shift = 64
    while shift >= games:
        x = x + pltpu.roll(x, shift, 1)
        shift //= 2
    return x


def spread_heads(given, games, amount):
    rows = [jnp.broadcast_to(given[d : d + 1, :], (games, CH)) for d in range(amount)]
    if games * amount < CH:
        rows.append(jnp.zeros((CH - games * amount, CH), F32))
    return jnp.concatenate(rows, axis=0).astype(BF16)


def own_lane(games):
    game = lax.broadcasted_iota(jnp.int32, (games, CH), 0)
    lane = lax.broadcasted_iota(jnp.int32, (games, CH), 1)
    return (lane % games == game).astype(F32)


def head_cells(h, heads, mine, games):
    out = lax.dot_general(h, heads[...], (((1,), (1,)), ((), ())), preferred_element_type=F32)
    return jnp.sum(out.reshape(ROWS * SIDE, games, CH) * mine[None], axis=1)


def advance(source, i, games, layer_weights):
    act = jnp.dot(columns(source, i, games, False), layer_weights, preferred_element_type=F32)
    return act, (inner(source, i, games).astype(F32) + jnp.maximum(act, 0.0)).astype(BF16)


def trace_terms(logits_ref, given, games):
    spread = lane_sum(given[8:16], games)
    action = spread[0:1].astype(jnp.int32)
    behave, regul, reward = spread[1:2], spread[2:3], spread[3:4]
    lane = lax.broadcasted_iota(jnp.int32, (1, CH), 1)
    slot = lane % games
    every = logits_ref[...]
    cell_id = lax.broadcasted_iota(jnp.int32, every.shape, 0) * SIDE + lax.broadcasted_iota(
        jnp.int32, every.shape, 1
    )
    lane_full = lax.broadcasted_iota(jnp.int32, every.shape, 2)
    policy_full = lane_full < 4 * games
    taken = (lane_full // games) * CELLS + cell_id == action.reshape(1, 1, CH)
    taken = jnp.where(policy_full, jnp.where(taken, 1.0, 0.0), 0.0)
    logits = jnp.where(policy_full, every, 0.0)

    def over_cells(x):
        return jnp.sum(jnp.sum(x, axis=0), axis=0, keepdims=True)

    exps = jnp.where(policy_full, jnp.exp(logits), 0.0)
    log_total = jnp.log(lane_sum(over_cells(exps), games))
    logp = lane_sum(over_cells(taken * logits), games) - log_total
    value_lane = jnp.where((lane >= 4 * games) & (lane < 5 * games), 1.0, 0.0)
    values = jnp.tanh(lane_sum(over_cells(every) * value_lane, games) / CELLS)

    def ahead(x, by):
        return jnp.where(slot + by < games, pltpu.roll(x, CH - by, 1), 0.0)

    length = given[5:6]
    place = slot.astype(F32)
    live = jnp.where(place < length, 1.0, 0.0)
    next_live = jnp.where(place + 1.0 < length, 1.0, 0.0)
    ratio = jnp.minimum(1.0, jnp.exp(logp - behave))
    shaped = reward - ETA * (logp - regul)
    delta = live * ratio * (shaped + ahead(values, 1) * next_live - values)
    correction, slope = live * delta, live * ratio
    by = 1
    while by < games:
        correction = correction + slope * ahead(correction, by)
        slope = slope * ahead(slope, by)
        by *= 2
    targets = values + correction
    policy_term = -live * ratio * (shaped + ahead(targets, 1) * next_live - values)
    value_term = -live * (targets - values)
    value_cell = value_term * (1.0 - values * values) / CELLS * value_lane
    probs = jnp.exp(logits - log_total.reshape(1, 1, CH))
    logits_ref[...] = jnp.where(
        policy_full,
        policy_term.reshape(1, 1, CH) * (taken - probs),
        jnp.broadcast_to(value_cell.reshape(1, 1, CH), logits.shape),
    )


def learner_part(given, grad, weights, scratch, after_half):
    hs, acts, turned, pre, hidden_grad, cells, heads, total = scratch
    games = 16
    block = ROWS * SIDE * games
    role = lax.axis_index("role")
    h0, h1, a0, a1 = hs.at[0], hs.at[1], acts.at[0], acts.at[1]
    heads[...] = spread_heads(given, games, 5)
    mine = own_lane(games)

    def layer_one(step, i):
        act, h = advance(h0, i, games, weights[0:TAPS])
        pre[0, pl.ds(pl.multiple_of(step * block, block), block)] = act
        set_inner(h1, i, games, h)

    steps(layer_one)

    def layer_two(step, i):
        act, h = advance(h1, i, games, weights[TAPS : 2 * TAPS])
        pre[1, pl.ds(pl.multiple_of(step * block, block), block)] = act
        cells[pl.ds(i, ROWS)] = head_cells(h, heads, mine, games).reshape(ROWS, SIDE, CH)

    steps(layer_two)
    trace_terms(cells, given, games)

    def top(step, i):
        at = pl.ds(pl.multiple_of(step * block, block), block)
        g = cells[pl.ds(i, ROWS)].reshape(ROWS * SIDE, 1, CH) * mine[None]
        g = g.reshape(block, CH)
        high = g.astype(BF16)
        low = (g - high.astype(F32)).astype(BF16)
        out = jnp.dot(high, heads[...], preferred_element_type=F32)
        out = out + jnp.dot(low, heads[...], preferred_element_type=F32)
        hidden_grad[at] = out
        set_inner(a1, i, games, jnp.where(pre[1, at] > 0, out, 0.0).astype(BF16))

    steps(top)

    @pl.when(role == 0)
    def _():
        for offset in range(9):
            at = TAPS + offset * CH
            turned[offset * CH : (offset + 1) * CH, :] = (
                weights[at : at + CH, :].astype(F32).T.astype(BF16)
            )

        def back(step, i):
            at = pl.ds(pl.multiple_of(step * block, block), block)
            out = hidden_grad[at] + jnp.dot(
                columns(a1, i, games, True), turned[...], preferred_element_type=F32
            )
            set_inner(a0, i, games, jnp.where(pre[0, at] > 0, out, 0.0).astype(BF16))

        steps(back)

    h, a = hs.at[role], acts.at[role]
    for half, (first, last) in enumerate(((0, 5), (5, 9))):
        lanes = slice(first * CH, last * CH)

        def product(i):
            return lax.dot_general(
                inner(h, i, games),
                columns(a, i, games, True, first, last),
                (((0,), (0,)), ((), ())),
                preferred_element_type=F32,
            )

        summed = product(0)
        for step in range(1, SIDE // ROWS):
            summed = summed + product(step * ROWS)
        for offset in range(first, last):
            at = (offset - first) * CH
            grad[offset * CH : (offset + 1) * CH, :] = summed[:, at : at + CH]
        after_half(half)


def learner_scratch():
    padded = (2, SIDE + 2, SIDE + 2, 16, CH)
    return [
        pltpu.VMEM(padded, BF16),
        pltpu.VMEM(padded, BF16),
        pltpu.VMEM((TAPS, CH), BF16),
        pltpu.VMEM((2, 1600, CH), F32),
        pltpu.VMEM((1600, CH), F32),
        pltpu.VMEM((SIDE, SIDE, CH), F32),
        pltpu.VMEM((CH, CH), BF16),
        pltpu.VMEM((8, CH), F32),
    ]


def actor_part(given, weights, scratch, games, out, start, ready):
    h0, h1, cells, heads = scratch
    heads[...] = spread_heads(given, games, 4)
    cells[...] = jnp.zeros(cells.shape, F32)
    mine = own_lane(games)
    ready(0)

    def layer_one(step, i):
        _, h = advance(h0, i, games, weights[0:TAPS])
        set_inner(h1, i, games, h)

    steps(layer_one)
    ready(1)

    def layer_two(step, i):
        _, h = advance(h1, i, games, weights[TAPS : 2 * TAPS])
        found = head_cells(h, heads, mine, games).reshape(ROWS, SIDE, CH)
        for part in range(ROWS):
            cells[pl.ds((i + part) * SIDE, SIDE), :] = found[part]

    steps(layer_two)
    logits = cells[...]
    cell_id = lax.broadcasted_iota(jnp.int32, logits.shape, 0)
    exps = jnp.where(cell_id < CELLS, jnp.exp(logits), 0.0)
    log_total = jnp.log(lane_sum(jnp.sum(exps, axis=0, keepdims=True), games))
    turned = (logits - log_total).T
    for d in range(4):
        out[pl.ds(start, games), d * CELLS : (d + 1) * CELLS] = turned[
            d * games : (d + 1) * games, 0:CELLS
        ]


def actor_scratch(games):
    padded = (SIDE + 2, SIDE + 2, games, CH)
    return [
        pltpu.VMEM(padded, BF16),
        pltpu.VMEM(padded, BF16),
        pltpu.VMEM((CH, CH), F32),
        pltpu.VMEM((CH, CH), BF16),
    ]


def learner_kernel(traj, given, torso, grad, weights, sem, *scratch):
    hs, acts = scratch[:2]
    for layer in range(2):
        clear_rim(hs.at[layer])
        clear_rim(acts.at[layer])
    copy = pltpu.make_async_copy(traj, center(hs.at[0]), sem)
    copy.start()
    weights[...] = torso[...].astype(BF16)
    copy.wait()
    learner_part(given, grad, weights, scratch, lambda half: None)


def learner(traj, given, torso):
    return pl.pallas_call(
        learner_kernel,
        out_shape=jax.ShapeDtypeStruct((TAPS, CH), F32),
        in_specs=[pl.BlockSpec(memory_space=pl.ANY), vmem(), vmem()],
        out_specs=vmem(),
        scratch_shapes=[pltpu.VMEM((2 * TAPS, CH), BF16), pltpu.SemaphoreType.DMA]
        + learner_scratch(),
        compiler_params=pltpu.CompilerParams(vmem_limit_bytes=48 << 20),
    )(traj, given, torso)


def actor_kernel(games, boards, given, torso, out, weights, sem, *scratch):
    h0, h1 = scratch[:2]
    clear_rim(h0)
    clear_rim(h1)
    start = pl.multiple_of(lax.axis_index("role") * games, games)
    copy = pltpu.make_async_copy(boards.at[:, :, pl.ds(start, games)], center(h0), sem)
    copy.start()
    weights[...] = torso[...].astype(BF16)
    copy.wait()
    actor_part(given, weights, scratch, games, out, 0, lambda layer: None)


def actor(boards, given, torso, games):
    return pl.pallas_call(
        functools.partial(actor_kernel, games),
        out_shape=jax.ShapeDtypeStruct((games, 4 * CELLS), F32),
        in_specs=[pl.BlockSpec(memory_space=pl.ANY), vmem(), vmem()],
        out_specs=vmem(),
        scratch_shapes=[pltpu.VMEM((2 * TAPS, CH), BF16), pltpu.SemaphoreType.DMA]
        + actor_scratch(games),
        compiler_params=pltpu.CompilerParams(vmem_limit_bytes=48 << 20),
    )(boards, given, torso)


def step_kernel(games, boards, traj, *refs):
    parts, (torso, moment_one, moment_two, share_out, out), scratch = refs[:7], refs[7:12], refs[12:]
    (weights, full, torso_in, one_in, two_in, grad, plane, quarter, line, norms) = scratch[:10]
    (s1, r1, s2, r2, sn, rn, sz, rz, sp, rp, ss, rs, loads, send_out, recv_out) = scratch[10:25]
    learner_refs, actor_refs = scratch[25:33], scratch[33:37]
    given, part_refs = scratch[37], scratch[38:]
    share = moment_one.shape[0]
    role = lax.axis_index("role")
    dp = lax.axis_index("dp")
    z, spot = dp // 4, dp % 4
    owner = z // 2 == role
    start = pl.multiple_of(role * games, games)

    def send(src, dst, send_sem, recv_sem, to_role, to_dp):
        copy = pltpu.make_async_remote_copy(
            src_ref=src,
            dst_ref=dst,
            send_sem=send_sem,
            recv_sem=recv_sem,
            device_id=(to_role, to_dp),
            device_id_type=MESH,
        )
        return copy

    barrier = pltpu.get_barrier_semaphore()

    def greet(to_role, to_dp):
        pl.semaphore_signal(barrier, inc=1, device_id=(to_role, to_dp), device_id_type=MESH)

    @pl.when(owner)
    def _():
        for k in range(1, 16):
            other = (dp + k) % 16
            greet(other // 8, other)
        for o in range(2):
            greet(role, (2 - 2 * role + o) * 4 + spot)
        greet(1 - role, dp)

    @pl.when(jnp.logical_not(owner))
    def _():
        for k in range(1, 4):
            greet(role, z * 4 + (spot + k) % 4)
            greet(role, ((z + k) % 4) * 4 + spot)
        greet(1 - role, dp)

    hs, acts = learner_refs[:2]
    clear_rim(hs.at[0])
    load_traj = pltpu.make_async_copy(traj, center(hs.at[0]), loads.at[0])
    load_torso = pltpu.make_async_copy(torso, torso_in, loads.at[1])
    load_one = pltpu.make_async_copy(moment_one, one_in, loads.at[2])
    load_two = pltpu.make_async_copy(moment_two, two_in, loads.at[3])
    load_torso.start()
    load_traj.start()
    clear_rim(actor_refs[0])
    load_boards = pltpu.make_async_copy(
        boards.at[:, :, pl.ds(start, games)], center(actor_refs[0]), loads.at[4]
    )
    load_parts = [
        pltpu.make_async_copy(part, ref, loads.at[5 + n])
        for n, (part, ref) in enumerate(zip(parts, part_refs))
    ]
    for load in load_parts:
        load.start()
    load_one.start()
    load_two.start()
    load_boards.start()
    clear_rim(hs.at[1])
    clear_rim(acts.at[0])
    clear_rim(acts.at[1])
    clear_rim(actor_refs[1])
    for load in load_parts:
        load.wait()
    policy_ref, value_ref, length_ref = part_refs[:3]
    given[...] = jnp.zeros(given.shape, F32)
    given[0:4, :] = policy_ref[...].astype(F32)
    given[4:5, :] = value_ref[...].astype(F32)
    given[5:6, :] = jnp.broadcast_to(length_ref[...].astype(F32), (1, CH))
    for n, ref in enumerate(part_refs[3:]):
        given[8 + n : 9 + n, 0:16] = ref[...].astype(F32)
    load_torso.wait()
    weights[...] = torso_in[...].astype(BF16)
    load_traj.wait()

    def rows(index):
        return pl.ds(pl.multiple_of(index * share, 8), share)

    def to_plane(o, k):
        p = (spot + k) % 4
        return send(
            grad.at[rows(4 * o + p)],
            plane.at[o, spot],
            s1.at[o, k - 1],
            r1.at[o, spot],
            role,
            z * 4 + p,
        )

    def from_plane(o, k):
        p = (spot + k) % 4
        return send(
            grad.at[rows(4 * o + p)], plane.at[o, p], s1.at[o, k - 1], r1.at[o, p], role, z * 4 + p
        )

    def after_half(half):
        if half == 0:

            @pl.when(owner)
            def _():
                pl.semaphore_wait(barrier, 18)

            @pl.when(jnp.logical_not(owner))
            def _():
                pl.semaphore_wait(barrier, 7)

        for k in range(1, 4):
            to_plane(half, k).start()

    learner_part(given, grad, weights, learner_refs, after_half)
    load_one.wait()
    load_two.wait()
    load_boards.wait()

    def to_owner(o):
        return send(
            quarter.at[o], line.at[z], s2.at[o], r2.at[z], role, (2 * role + o) * 4 + spot
        )

    for o in range(2):
        summed = grad[rows(4 * o + spot)]
        for k in range(1, 4):
            from_plane(o, k).wait_recv()
            summed = summed + plane[o, (spot + k) % 4]
        quarter[o] = summed

        @pl.when(z != 2 * role + o)
        def _():
            to_owner(o).start()

    def to_peer(o, k):
        p = (spot + k) % 4
        at = full.at[rows((2 * role + o) * 4 + spot)]
        return send(at, at, sp.at[o, k - 1], rp.at[o, spot], role, z * 4 + p)

    def to_sibling(o, k):
        p = (spot + k) % 4
        at = full.at[rows((2 * role + o) * 4 + p)]
        return send(at, at, ss.at[o, k], rs.at[o, p], 1 - role, dp)

    def to_norm(k):
        other = (dp + k) % 16
        return send(norms.at[dp], norms.at[dp], sn.at[k - 1], rn.at[dp], other // 8, other)

    def from_norm(k):
        other = (dp + k) % 16
        return send(norms.at[other], norms.at[other], sn.at[k - 1], rn.at[other], other // 8, other)

    def down_line(k):
        return send(
            full.at[rows(dp)],
            full.at[rows(dp)],
            sz.at[k - 1],
            rz.at[z % 2],
            role,
            ((z + k) % 4) * 4 + spot,
        )

    @pl.when(owner)
    def _():
        summed = quarter[z % 2]
        for k in range(1, 4):
            other = (z + k) % 4
            send(
                quarter.at[0], line.at[other], s2.at[0], r2.at[other], role, other * 4 + spot
            ).wait_recv()
            summed = summed + line[other]
        norms[dp] = jnp.sum((summed * summed).reshape(share // 8, 8, CH), axis=0)
        for k in range(1, 16):
            to_norm(k).start()
        for k in range(1, 16):
            from_norm(k).wait_recv()
        square_sum = jnp.sum(jnp.sum(norms[...], axis=0), axis=0, keepdims=True)
        square_sum = jnp.sum(square_sum, axis=1, keepdims=True)
        size = float(torso.shape[0] * torso.shape[1])
        factor = jnp.minimum(1.0, jnp.sqrt(jnp.full((1, 1), size, F32)) / jnp.sqrt(square_sum + NORM_EPS))
        clipped = summed * factor
        one = BETA_ONE * one_in[...] + (1.0 - BETA_ONE) * clipped
        two = BETA_TWO * two_in[...] + (1.0 - BETA_TWO) * clipped * clipped
        full[rows(dp)] = torso_in[rows(dp)] - LEARN_RATE * one / (jnp.sqrt(two) + ADAM_EPS)
        for k in range(1, 4):
            down_line(k).start()
        for k in range(1, 4):
            to_peer(z % 2, k).start()
        to_sibling(z % 2, 0).start()

    for o in range(2):
        at = full.at[rows((2 * role + o) * 4 + spot)]

        @pl.when(z != 2 * role + o)
        def _():
            send(at, at, sz.at[0], rz.at[o], role, (2 * role + o) * 4 + spot).wait_recv()
            for k in range(1, 4):
                to_peer(o, k).start()
            to_sibling(o, 0).start()

    for o in range(2):
        for k in range(1, 4):
            p = (spot + k) % 4
            at = full.at[rows((2 * role + o) * 4 + p)]
            send(at, at, sp.at[o, k - 1], rp.at[o, p], role, z * 4 + p).wait_recv()
            to_sibling(o, k).start()

    def from_sibling():
        for o in range(2):
            for p in range(4):
                at = full.at[rows((2 - 2 * role + o) * 4 + p)]
                send(at, at, ss.at[o, p], rs.at[o, p], 1 - role, dp).wait_recv()

    def ready(layer):
        @pl.when(role == 1 - layer)
        def _():
            from_sibling()

        at = slice(layer * TAPS, (layer + 1) * TAPS)
        weights[at, :] = full[at, :].astype(BF16)

    actor_part(given, weights, actor_refs, games, out, start, ready)
    share_out[...] = full[rows(dp)]
    mine = out.at[pl.ds(start, games)]
    send(mine, mine, send_out, recv_out, 1 - role, dp).start()
    theirs = out.at[pl.ds(pl.multiple_of((1 - role) * games, games), games)]
    send(mine, theirs, send_out, recv_out, 1 - role, dp).wait_recv()
    send(mine, mine, send_out, recv_out, 1 - role, dp).wait_send()
    for o in range(2):
        for k in range(1, 4):
            to_plane(o, k).wait_send()
            to_peer(o, k).wait_send()
        for k in range(4):
            to_sibling(o, k).wait_send()

        @pl.when(z != 2 * role + o)
        def _():
            to_owner(o).wait_send()

    @pl.when(owner)
    def _():
        for k in range(1, 16):
            to_norm(k).wait_send()
        for k in range(1, 4):
            down_line(k).wait_send()


def step_call(boards, traj, parts, torso, moment_one, moment_two):
    share, games = moment_one.shape[0], boards.shape[2] // 2
    dma = pltpu.SemaphoreType.DMA
    return pl.pallas_call(
        functools.partial(step_kernel, games),
        out_shape=(
            jax.ShapeDtypeStruct((share, CH), F32),
            jax.ShapeDtypeStruct((2 * games, 4 * CELLS), F32),
        ),
        in_specs=[pl.BlockSpec(memory_space=pl.ANY) for _ in range(12)],
        out_specs=(vmem(), vmem()),
        scratch_shapes=[
            pltpu.VMEM((2 * TAPS, CH), BF16),
            pltpu.VMEM((2 * TAPS, CH), F32),
            pltpu.VMEM((2 * TAPS, CH), F32),
            pltpu.VMEM((share, CH), F32),
            pltpu.VMEM((share, CH), F32),
            pltpu.VMEM((TAPS, CH), F32),
            pltpu.VMEM((2, 4, share, CH), F32),
            pltpu.VMEM((2, share, CH), F32),
            pltpu.VMEM((4, share, CH), F32),
            pltpu.VMEM((16, 8, CH), F32),
            dma((2, 3)),
            dma((2, 4)),
            dma((2,)),
            dma((4,)),
            dma((15,)),
            dma((16,)),
            dma((3,)),
            dma((2,)),
            dma((2, 3)),
            dma((2, 4)),
            dma((2, 4)),
            dma((2, 4)),
            dma((12,)),
            dma,
            dma,
        ]
        + learner_scratch()
        + actor_scratch(games)
        + [pltpu.VMEM((16, CH), F32)]
        + [pltpu.VMEM(part.shape, part.dtype) for part in parts],
        compiler_params=pltpu.CompilerParams(
            collective_id=0, has_side_effects=True, vmem_limit_bytes=56 << 20
        ),
    )(boards, traj, *parts, torso, moment_one, moment_two)


def update_any(grad, torso, moment_one, moment_two):
    share = moment_one.shape[0]
    summed = lax.all_gather(lax.psum(grad, "dp"), "role", axis=0, tiled=True)
    start = lax.axis_index("dp") * share
    square_sum = jnp.sum(summed * summed)
    factor = jnp.minimum(1.0, jnp.sqrt(float(summed.size)) / jnp.sqrt(square_sum + NORM_EPS))
    clipped = lax.dynamic_slice_in_dim(summed, start, share, 0) * factor
    one = BETA_ONE * moment_one + (1.0 - BETA_ONE) * clipped
    two = BETA_TWO * moment_two + (1.0 - BETA_TWO) * clipped * clipped
    old = lax.dynamic_slice_in_dim(torso, start, share, 0)
    new = old - LEARN_RATE * one / (jnp.sqrt(two) + ADAM_EPS)
    return lax.all_gather(new, "dp", axis=0, tiled=True)


def join_kernel(part, out, send_sem, recv_sem):
    games = part.shape[0]
    role = lax.axis_index("role")
    dp = lax.axis_index("dp")
    barrier = pltpu.get_barrier_semaphore()
    pl.semaphore_signal(barrier, inc=1, device_id=(1 - role, dp), device_id_type=MESH)
    pl.semaphore_wait(barrier, 1)
    mine = pl.ds(pl.multiple_of(role * games, 8), games)
    copy = pltpu.make_async_remote_copy(
        src_ref=part,
        dst_ref=out.at[mine],
        send_sem=send_sem,
        recv_sem=recv_sem,
        device_id=(1 - role, dp),
        device_id_type=MESH,
    )
    copy.start()
    out[mine] = part[...]
    copy.wait()


def join(part):
    return pl.pallas_call(
        join_kernel,
        out_shape=jax.ShapeDtypeStruct((2 * part.shape[0], part.shape[1]), F32),
        in_specs=[vmem()],
        out_specs=vmem(),
        scratch_shapes=[pltpu.SemaphoreType.DMA, pltpu.SemaphoreType.DMA],
        compiler_params=pltpu.CompilerParams(collective_id=1, has_side_effects=True),
    )(part)


def body(
    board_now,
    traj_boards,
    actions,
    lengths,
    behaviour,
    regular,
    rewards,
    torso,
    policy_head,
    value_head,
    first_moment,
    second_moment,
):
    boards = jnp.transpose(board_now, (1, 2, 0, 3))
    traj = jnp.transpose(traj_boards[0], (1, 2, 0, 3))
    if lax.axis_size("dp") == 16 and lax.axis_size("role") == 2:
        parts = (policy_head.T, value_head[None, :], lengths[:, None])
        parts = parts + (actions, behaviour, regular, rewards)
        return step_call(boards, traj, parts, torso, first_moment, second_moment)

    def wide(x):
        return jnp.pad(x.astype(F32), ((0, 0), (0, CH - x.shape[1])))

    given = jnp.concatenate(
        [
            policy_head.T.astype(F32),
            value_head[None, :].astype(F32),
            jnp.broadcast_to(lengths.astype(F32)[:, None], (1, CH)),
            jnp.zeros((2, CH), F32),
            wide(actions),
            wide(behaviour),
            wide(regular),
            wide(rewards),
            jnp.zeros((4, CH), F32),
        ],
        axis=0,
    )
    grad = learner(traj, given, torso)
    weights = update_any(grad, torso, first_moment, second_moment)
    share_rows = first_moment.shape[0]
    start = lax.axis_index("dp") * share_rows
    new_share = lax.dynamic_slice_in_dim(weights, start, share_rows, 0)
    part = actor(boards, given, weights, board_now.shape[0] // 2)
    return (new_share, join(part))


def solution(mesh):
    return jax.shard_map(
        body,
        mesh=mesh,
        in_specs=(
            P("dp", None, None, None),
            P("dp", None, None, None, None),
            P("dp", None),
            P("dp"),
            P("dp", None),
            P("dp", None),
            P("dp", None),
            P(),
            P(),
            P(),
            P("dp", None),
            P("dp", None),
        ),
        out_specs=(P("dp", None), P("dp", None)),
        check_vma=False,
    )
```

time: 70.3 us -> 50 us (0.71)
  the two profiles are of different devices: /device:TPU:9 before, /device:TPU:0 now
where the time goes in v2:
time: 50 us; the launch traced here: 49.7 us
  Pallas kernels  45.4 us (91%)
  local copies, waits for them, and re-layouts  3.09 us (6%)
  between operations  1.29 us (3%)
    pallas_call x1, Pallas kernels, step_call(): pl.pallas_call(functools.partial(step_kernel, games), out_shape=(jax.Shap...  45.4 us
    unnamed x2, local copies, waits for them, and re-layouts  3.09 us

profile of v2, /device:TPU:0, one launch (start us, length us, event | category | flops | bytes accessed | tf_op | source)
XLA Modules:
  0.0 49.7 jit_solution(105782685495765782)
XLA Ops:
  1.3 45.4 %shard_map.131 = (f32[144,128]{1,0:T(8,128)}, f32[64,400]{1,0:T(8,128)}) custom-call(bf16[10,10,64,128]{3,2,1,0:T(8,128)(2,1)} %bitcast.8, bf16[10,10,16,128]{3,2,1,0:T(8,128)(2,1)} %bitcast.9, bf16[4,128]{1,0:T(4,128)(2,1)} %bitcast.10, bf16[1,128]{1,0:T(2,128)(2,1)} %bitcast.11, s32[1,1]{1,0:T(1,128)} %bitcast.7.refs_2_, s32[1,16]{1,0:T(1,128)} %refs_3_.1, ...), custom_call_target="tpu_custom_call" | custom-call | tf_op jit(solution)/shard_map/pallas_call | solution.py:586
  46.7 1.5 %copy.17 = f32[144,128]{1,0:T(8,128)} copy(f32[144,128]{1,0:T(8,128)} %get-tuple-element.4) | data formatting | bytes 147456
  48.2 1.6 %copy.18 = f32[64,400]{1,0:T(8,128)} copy(f32[64,400]{1,0:T(8,128)} %get-tuple-element.5) | data formatting | bytes 204800

commit v3 on v2

--- a/solution.py
+++ b/solution.py
@@ -17,6 +17,7 @@
 CELLS = 100
 CH = 128
 TAPS = 9 * CH
+PACKED = 12 * CH
 ROWS = 5
 F32 = jnp.float32
 BF16 = jnp.bfloat16
@@ -37,6 +38,42 @@
     return jnp.concatenate(parts, axis=1)
 
 
+def pair_columns(padded, i, games):
+    parts = []
+    for p in range(3):
+        for u in range(4):
+            cells = [
+                padded[pl.ds(i + p, ROWS), u + 2 * m : u + 2 * m + 1] for m in range(SIDE // 2)
+            ]
+            parts.append(jnp.concatenate(cells, axis=1).reshape(ROWS * SIDE // 2 * games, CH))
+    return jnp.concatenate(parts, axis=1)
+
+
+def pair_dot(padded, i, games, packed):
+    both = jnp.dot(pair_columns(padded, i, games), packed, preferred_element_type=F32)
+    shape = (ROWS, SIDE // 2, 1, games, CH)
+    halves = [both[:, 0:CH].reshape(shape), both[:, CH : 2 * CH].reshape(shape)]
+    return jnp.concatenate(halves, axis=2).reshape(ROWS * SIDE * games, CH)
+
+
+def pack(packed, blocks, back=False):
+    for offset in range(9):
+        p, q = offset // 3, offset % 3
+        block = blocks(offset)
+        for cell in range(2):
+            row, u = (2 - p, cell + 2 - q) if back else (p, q + cell)
+            at = (row * 4 + u) * CH
+            packed[at : at + CH, cell * CH : (cell + 1) * CH] = block
+
+
+def pack_layer(weights, torso, layer):
+    def block(offset):
+        at = layer * TAPS + offset * CH
+        return torso[at : at + CH, :].astype(BF16)
+
+    pack(weights.at[layer], block)
+
+
 def inner(padded, i, games):
     return padded[pl.ds(i + 1, ROWS), 1 : 1 + SIDE].reshape(ROWS * SIDE * games, CH)
 
@@ -59,11 +96,8 @@
 
 
 def steps(f):
-    def one(step, carry):
+    for step in range(SIDE // ROWS):
         f(step, step * ROWS)
-        return carry
-
-    lax.fori_loop(0, SIDE // ROWS, one, 0)
 
 
 def lane_sum(x, games):
@@ -93,7 +127,7 @@
 
 
 def advance(source, i, games, layer_weights):
-    act = jnp.dot(columns(source, i, games, False), layer_weights, preferred_element_type=F32)
+    act = pair_dot(source, i, games, layer_weights[...])
     return act, (inner(source, i, games).astype(F32) + jnp.maximum(act, 0.0)).astype(BF16)
 
 
@@ -150,34 +184,34 @@
     )
 
 
-def learner_part(given, grad, weights, scratch, after_half):
+def learner_part(given, torso, grad, weights, scratch, after_half):
     hs, acts, turned, pre, hidden_grad, cells, heads, total = scratch
     games = 16
-    block = ROWS * SIDE * games
+    size = ROWS * SIDE * games
     role = lax.axis_index("role")
     h0, h1, a0, a1 = hs.at[0], hs.at[1], acts.at[0], acts.at[1]
     heads[...] = spread_heads(given, games, 5)
     mine = own_lane(games)
 
     def layer_one(step, i):
-        act, h = advance(h0, i, games, weights[0:TAPS])
-        pre[0, pl.ds(pl.multiple_of(step * block, block), block)] = act
+        act, h = advance(h0, i, games, weights.at[0])
+        pre[0, pl.ds(step * size, size)] = act
         set_inner(h1, i, games, h)
 
     steps(layer_one)
 
     def layer_two(step, i):
-        act, h = advance(h1, i, games, weights[TAPS : 2 * TAPS])
-        pre[1, pl.ds(pl.multiple_of(step * block, block), block)] = act
+        act, h = advance(h1, i, games, weights.at[1])
+        pre[1, pl.ds(step * size, size)] = act
         cells[pl.ds(i, ROWS)] = head_cells(h, heads, mine, games).reshape(ROWS, SIDE, CH)
 
     steps(layer_two)
     trace_terms(cells, given, games)
 
     def top(step, i):
-        at = pl.ds(pl.multiple_of(step * block, block), block)
+        at = pl.ds(step * size, size)
         g = cells[pl.ds(i, ROWS)].reshape(ROWS * SIDE, 1, CH) * mine[None]
-        g = g.reshape(block, CH)
+        g = g.reshape(size, CH)
         high = g.astype(BF16)
         low = (g - high.astype(F32)).astype(BF16)
         out = jnp.dot(high, heads[...], preferred_element_type=F32)
@@ -189,17 +223,17 @@
 
     @pl.when(role == 0)
     def _():
-        for offset in range(9):
+        turned[...] = jnp.zeros(turned.shape, BF16)
+
+        def block(offset):
             at = TAPS + offset * CH
-            turned[offset * CH : (offset + 1) * CH, :] = (
-                weights[at : at + CH, :].astype(F32).T.astype(BF16)
-            )
+            return torso[at : at + CH, :].T.astype(BF16)
+
+        pack(turned, block, True)
 
         def back(step, i):
-            at = pl.ds(pl.multiple_of(step * block, block), block)
-            out = hidden_grad[at] + jnp.dot(
-                columns(a1, i, games, True), turned[...], preferred_element_type=F32
-            )
+            at = pl.ds(step * size, size)
+            out = hidden_grad[at] + pair_dot(a1, i, games, turned[...])
             set_inner(a0, i, games, jnp.where(pre[0, at] > 0, out, 0.0).astype(BF16))
 
         steps(back)
@@ -230,7 +264,7 @@
     return [
         pltpu.VMEM(padded, BF16),
         pltpu.VMEM(padded, BF16),
-        pltpu.VMEM((TAPS, CH), BF16),
+        pltpu.VMEM((PACKED, 2 * CH), BF16),
         pltpu.VMEM((2, 1600, CH), F32),
         pltpu.VMEM((1600, CH), F32),
         pltpu.VMEM((SIDE, SIDE, CH), F32),
@@ -247,14 +281,14 @@
     ready(0)
 
     def layer_one(step, i):
-        _, h = advance(h0, i, games, weights[0:TAPS])
+        _, h = advance(h0, i, games, weights.at[0])
         set_inner(h1, i, games, h)
 
     steps(layer_one)
     ready(1)
 
     def layer_two(step, i):
-        _, h = advance(h1, i, games, weights[TAPS : 2 * TAPS])
+        _, h = advance(h1, i, games, weights.at[1])
         found = head_cells(h, heads, mine, games).reshape(ROWS, SIDE, CH)
         for part in range(ROWS):
             cells[pl.ds((i + part) * SIDE, SIDE), :] = found[part]
@@ -288,9 +322,11 @@
         clear_rim(acts.at[layer])
     copy = pltpu.make_async_copy(traj, center(hs.at[0]), sem)
     copy.start()
-    weights[...] = torso[...].astype(BF16)
+    weights[...] = jnp.zeros(weights.shape, BF16)
+    for layer in range(2):
+        pack_layer(weights, torso, layer)
     copy.wait()
-    learner_part(given, grad, weights, scratch, lambda half: None)
+    learner_part(given, torso, grad, weights, scratch, lambda half: None)
 
 
 def learner(traj, given, torso):
@@ -299,7 +335,7 @@
         out_shape=jax.ShapeDtypeStruct((TAPS, CH), F32),
         in_specs=[pl.BlockSpec(memory_space=pl.ANY), vmem(), vmem()],
         out_specs=vmem(),
-        scratch_shapes=[pltpu.VMEM((2 * TAPS, CH), BF16), pltpu.SemaphoreType.DMA]
+        scratch_shapes=[pltpu.VMEM((2, PACKED, 2 * CH), BF16), pltpu.SemaphoreType.DMA]
         + learner_scratch(),
         compiler_params=pltpu.CompilerParams(vmem_limit_bytes=48 << 20),
     )(traj, given, torso)
@@ -312,7 +348,9 @@
     start = pl.multiple_of(lax.axis_index("role") * games, games)
     copy = pltpu.make_async_copy(boards.at[:, :, pl.ds(start, games)], center(h0), sem)
     copy.start()
-    weights[...] = torso[...].astype(BF16)
+    weights[...] = jnp.zeros(weights.shape, BF16)
+    for layer in range(2):
+        pack_layer(weights, torso, layer)
     copy.wait()
     actor_part(given, weights, scratch, games, out, 0, lambda layer: None)
 
@@ -323,7 +361,7 @@
         out_shape=jax.ShapeDtypeStruct((games, 4 * CELLS), F32),
         in_specs=[pl.BlockSpec(memory_space=pl.ANY), vmem(), vmem()],
         out_specs=vmem(),
-        scratch_shapes=[pltpu.VMEM((2 * TAPS, CH), BF16), pltpu.SemaphoreType.DMA]
+        scratch_shapes=[pltpu.VMEM((2, PACKED, 2 * CH), BF16), pltpu.SemaphoreType.DMA]
         + actor_scratch(games),
         compiler_params=pltpu.CompilerParams(vmem_limit_bytes=48 << 20),
     )(boards, given, torso)
@@ -408,8 +446,10 @@
     given[5:6, :] = jnp.broadcast_to(length_ref[...].astype(F32), (1, CH))
     for n, ref in enumerate(part_refs[3:]):
         given[8 + n : 9 + n, 0:16] = ref[...].astype(F32)
+    weights[...] = jnp.zeros(weights.shape, BF16)
     load_torso.wait()
-    weights[...] = torso_in[...].astype(BF16)
+    for layer in range(2):
+        pack_layer(weights, torso_in, layer)
     load_traj.wait()
 
     def rows(index):
@@ -446,7 +486,7 @@
         for k in range(1, 4):
             to_plane(half, k).start()
 
-    learner_part(given, grad, weights, learner_refs, after_half)
+    learner_part(given, torso_in, grad, weights, learner_refs, after_half)
     load_one.wait()
     load_two.wait()
     load_boards.wait()
@@ -551,11 +591,12 @@
         def _():
             from_sibling()
 
-        at = slice(layer * TAPS, (layer + 1) * TAPS)
-        weights[at, :] = full[at, :].astype(BF16)
+        pack_layer(weights, full, layer)
 
     actor_part(given, weights, actor_refs, games, out, start, ready)
-    share_out[...] = full[rows(dp)]
+    share_out[0:share] = full[rows(dp)]
+    share_out[share : share + 8] = jnp.zeros((8, CH), F32)
+    out[2 * games : 2 * games + 8] = jnp.zeros((8, 4 * CELLS), F32)
     mine = out.at[pl.ds(start, games)]
     send(mine, mine, send_out, recv_out, 1 - role, dp).start()
     theirs = out.at[pl.ds(pl.multiple_of((1 - role) * games, games), games)]
@@ -586,13 +627,13 @@
     return pl.pallas_call(
         functools.partial(step_kernel, games),
         out_shape=(
-            jax.ShapeDtypeStruct((share, CH), F32),
-            jax.ShapeDtypeStruct((2 * games, 4 * CELLS), F32),
+            jax.ShapeDtypeStruct((share + 8, CH), F32),
+            jax.ShapeDtypeStruct((2 * games + 8, 4 * CELLS), F32),
         ),
         in_specs=[pl.BlockSpec(memory_space=pl.ANY) for _ in range(12)],
         out_specs=(vmem(), vmem()),
         scratch_shapes=[
-            pltpu.VMEM((2 * TAPS, CH), BF16),
+            pltpu.VMEM((2, PACKED, 2 * CH), BF16),
             pltpu.VMEM((2 * TAPS, CH), F32),
             pltpu.VMEM((2 * TAPS, CH), F32),
             pltpu.VMEM((share, CH), F32),
@@ -693,7 +734,8 @@
     if lax.axis_size("dp") == 16 and lax.axis_size("role") == 2:
         parts = (policy_head.T, value_head[None, :], lengths[:, None])
         parts = parts + (actions, behaviour, regular, rewards)
-        return step_call(boards, traj, parts, torso, first_moment, second_moment)
+        new_share, logp = step_call(boards, traj, parts, torso, first_moment, second_moment)
+        return (new_share[: first_moment.shape[0]], logp[: board_now.shape[0]])
 
     def wide(x):
         return jnp.pad(x.astype(F32), ((0, 0), (0, CH - x.shape[1])))

time: 50 us -> 48.6 us (0.972)
  Pallas kernels: 45.4 us -> 44 us
    slice x0 -> x2, local copies, waits for them, and re-layouts: none -> 3.09 us  [body(): return (new_share[:first_moment.shape[0]], logp[:board_now.shape[0]])]
    unnamed x2 -> x0, local copies, waits for them, and re-layouts: 3.09 us -> none
    pallas_call x1, Pallas kernels: 45.4 us -> 44 us  [step_call(): pl.pallas_call(functools.partial(step_kernel, games), out_shape=(jax.Shap...]
where the time goes in v3:
time: 48.6 us; the launch traced here: 48.4 us
  Pallas kernels  44 us (91%)
  local copies, waits for them, and re-layouts  3.09 us (6%)
  between operations  1.29 us (3%)
    pallas_call x1, Pallas kernels, step_call(): pl.pallas_call(functools.partial(step_kernel, games), out_shape=(jax.Shap...  44 us
    slice x2, local copies, waits for them, and re-layouts, body(): return (new_share[:first_moment.shape[0]], logp[:board_now.shape[0]])  3.09 us

profile of v3, /device:TPU:0, one launch (start us, length us, event | category | flops | bytes accessed | tf_op | source)
XLA Modules:
  0.0 48.4 jit_solution(10269834228564939476)
XLA Ops:
  1.3 44.0 %shard_map.131 = (f32[152,128]{1,0:T(8,128)}, f32[72,400]{1,0:T(8,128)}) custom-call(bf16[10,10,64,128]{3,2,1,0:T(8,128)(2,1)} %bitcast.8, bf16[10,10,16,128]{3,2,1,0:T(8,128)(2,1)} %bitcast.9, bf16[4,128]{1,0:T(4,128)(2,1)} %bitcast.10, bf16[1,128]{1,0:T(2,128)(2,1)} %bitcast.11, s32[1,1]{1,0:T(1,128)} %bitcast.7.refs_2_, s32[1,16]{1,0:T(1,128)} %refs_3_.1, ...), custom_call_target="tpu_custom_call" | custom-call | tf_op jit(solution)/shard_map/pallas_call | solution.py:627
  45.3 1.5 %slice.6 = f32[144,128]{1,0:T(8,128)} slice(f32[152,128]{1,0:T(8,128)} %get-tuple-element.4), slice={[0:144], [0:128]} | slice | bytes 147456 | tf_op jit(solution)/shard_map/slice | solution.py:738
  46.8 1.6 %slice.7 = f32[64,400]{1,0:T(8,128)} slice(f32[72,400]{1,0:T(8,128)} %get-tuple-element.5), slice={[0:64], [0:400]} | slice | bytes 204800 | tf_op jit(solution)/shard_map/slice | solution.py:738

commit v4 on v3

--- a/solution.py
+++ b/solution.py
@@ -26,16 +26,6 @@
 
 def vmem():
     return pl.BlockSpec(memory_space=pltpu.VMEM)
-
-
-def columns(padded, i, games, flip, first=0, last=9):
-    parts = []
-    for offset in range(first, last):
-        p, q = offset // 3, offset % 3
-        u, v = (2 - p, 2 - q) if flip else (p, q)
-        window = padded[pl.ds(i + u, ROWS), v : v + SIDE]
-        parts.append(window.reshape(ROWS * SIDE * games, CH))
-    return jnp.concatenate(parts, axis=1)
 
 
 def pair_columns(padded, i, games):
@@ -239,23 +229,20 @@
         steps(back)
 
     h, a = hs.at[role], acts.at[role]
-    for half, (first, last) in enumerate(((0, 5), (5, 9))):
-        lanes = slice(first * CH, last * CH)
-
-        def product(i):
-            return lax.dot_general(
-                inner(h, i, games),
-                columns(a, i, games, True, first, last),
-                (((0,), (0,)), ((), ())),
-                preferred_element_type=F32,
-            )
-
-        summed = product(0)
-        for step in range(1, SIDE // ROWS):
-            summed = summed + product(step * ROWS)
-        for offset in range(first, last):
-            at = (offset - first) * CH
-            grad[offset * CH : (offset + 1) * CH, :] = summed[:, at : at + CH]
+    right = [a[1 : SIDE + 1, 2 - q : 2 - q + SIDE].reshape(SIDE * SIDE * games, CH) for q in range(3)]
+    right = jnp.concatenate(right, axis=1)
+    for half, taps in enumerate(((0, 1), (2,))):
+        left = [h[p : p + SIDE, 1 : SIDE + 1].reshape(SIDE * SIDE * games, CH) for p in taps]
+        found = lax.dot_general(
+            jnp.concatenate(left, axis=1),
+            right,
+            (((0,), (0,)), ((), ())),
+            preferred_element_type=F32,
+        )
+        for n, p in enumerate(taps):
+            for q in range(3):
+                at = (3 * p + q) * CH
+                grad[at : at + CH, :] = found[n * CH : (n + 1) * CH, q * CH : (q + 1) * CH]
         after_half(half)
 
 
@@ -370,9 +357,9 @@
 def step_kernel(games, boards, traj, *refs):
     parts, (torso, moment_one, moment_two, share_out, out), scratch = refs[:7], refs[7:12], refs[12:]
     (weights, full, torso_in, one_in, two_in, grad, plane, quarter, line, norms) = scratch[:10]
-    (s1, r1, s2, r2, sn, rn, sz, rz, sp, rp, ss, rs, loads, send_out, recv_out) = scratch[10:25]
-    learner_refs, actor_refs = scratch[25:33], scratch[33:37]
-    given, part_refs = scratch[37], scratch[38:]
+    (s1, r1, s2, r2, sn, rn, sz, rz, sp, rp, ss, rs, sc, rc, loads, send_out, recv_out) = scratch[10:27]
+    learner_refs, actor_refs = scratch[27:35], scratch[35:39]
+    given, part_refs = scratch[39], scratch[40:]
     share = moment_one.shape[0]
     role = lax.axis_index("role")
     dp = lax.axis_index("dp")
@@ -507,15 +494,37 @@
         def _():
             to_owner(o).start()
 
-    def to_peer(o, k):
-        p = (spot + k) % 4
-        at = full.at[rows((2 * role + o) * 4 + spot)]
-        return send(at, at, sp.at[o, k - 1], rp.at[o, spot], role, z * 4 + p)
-
-    def to_sibling(o, k):
-        p = (spot + k) % 4
-        at = full.at[rows((2 * role + o) * 4 + p)]
-        return send(at, at, ss.at[o, k], rs.at[o, p], 1 - role, dp)
+    half = share // 2
+    near = (spot + 1 - 2 * (spot % 2), (spot + 2) % 4)
+    places = (spot,) + near + (3 - spot,)
+
+    def share_of(o, place, to_role=None):
+        group = role if to_role is None else to_role
+        return full.at[rows((2 * group + o) * 4 + place)]
+
+    def half_of(o, place, part):
+        begin = ((2 * role + o) * 4 + place) * share + part * half
+        return full.at[pl.ds(pl.multiple_of(begin, 8), half)]
+
+    def to_near(o, a):
+        at = share_of(o, spot)
+        return send(at, at, sp.at[o, a], rp.at[o, a], role, z * 4 + near[a])
+
+    def from_near(o, a):
+        at = share_of(o, near[a])
+        return send(at, at, sp.at[o, a], rp.at[o, a], role, z * 4 + near[a])
+
+    def to_corner(o, a):
+        at = half_of(o, near[a], a)
+        return send(at, at, sc.at[o, a], rc.at[o, a], role, z * 4 + near[1 - a])
+
+    def from_corner(o, a):
+        at = half_of(o, 3 - spot, a)
+        return send(at, at, sc.at[o, a], rc.at[o, a], role, z * 4 + near[1 - a])
+
+    def to_sibling(o, n):
+        at = share_of(o, places[n])
+        return send(at, at, ss.at[o, n], rs.at[o, n], 1 - role, dp)
 
     def to_norm(k):
         other = (dp + k) % 16
@@ -559,32 +568,37 @@
         full[rows(dp)] = torso_in[rows(dp)] - LEARN_RATE * one / (jnp.sqrt(two) + ADAM_EPS)
         for k in range(1, 4):
             down_line(k).start()
-        for k in range(1, 4):
-            to_peer(z % 2, k).start()
+        for a in range(2):
+            to_near(z % 2, a).start()
         to_sibling(z % 2, 0).start()
 
-    for o in range(2):
-        at = full.at[rows((2 * role + o) * 4 + spot)]
+    same = 1 - (z // 2 + role - 2 * (z // 2) * role)
+    first = same * (z % 2) + (1 - same) * (1 - role)
+    for o in (first, 1 - first):
 
         @pl.when(z != 2 * role + o)
         def _():
+            at = share_of(o, spot)
             send(at, at, sz.at[0], rz.at[o], role, (2 * role + o) * 4 + spot).wait_recv()
-            for k in range(1, 4):
-                to_peer(o, k).start()
+            for a in range(2):
+                to_near(o, a).start()
             to_sibling(o, 0).start()
 
-    for o in range(2):
-        for k in range(1, 4):
-            p = (spot + k) % 4
-            at = full.at[rows((2 * role + o) * 4 + p)]
-            send(at, at, sp.at[o, k - 1], rp.at[o, p], role, z * 4 + p).wait_recv()
-            to_sibling(o, k).start()
+    for o in (first, 1 - first):
+        for a in range(2):
+            from_near(o, a).wait_recv()
+            to_corner(o, a).start()
+            to_sibling(o, 1 + a).start()
+    for o in (first, 1 - first):
+        for a in range(2):
+            from_corner(o, a).wait_recv()
+        to_sibling(o, 3).start()
 
     def from_sibling():
         for o in range(2):
-            for p in range(4):
-                at = full.at[rows((2 - 2 * role + o) * 4 + p)]
-                send(at, at, ss.at[o, p], rs.at[o, p], 1 - role, dp).wait_recv()
+            for n in range(4):
+                at = share_of(o, places[n], 1 - role)
+                send(at, at, ss.at[o, n], rs.at[o, n], 1 - role, dp).wait_recv()
 
     def ready(layer):
         @pl.when(role == 1 - layer)
@@ -594,9 +608,7 @@
         pack_layer(weights, full, layer)
 
     actor_part(given, weights, actor_refs, games, out, start, ready)
-    share_out[0:share] = full[rows(dp)]
-    share_out[share : share + 8] = jnp.zeros((8, CH), F32)
-    out[2 * games : 2 * games + 8] = jnp.zeros((8, 4 * CELLS), F32)
+    share_out[...] = full[rows(dp)]
     mine = out.at[pl.ds(start, games)]
     send(mine, mine, send_out, recv_out, 1 - role, dp).start()
     theirs = out.at[pl.ds(pl.multiple_of((1 - role) * games, games), games)]
@@ -605,7 +617,9 @@
     for o in range(2):
         for k in range(1, 4):
             to_plane(o, k).wait_send()
-            to_peer(o, k).wait_send()
+        for a in range(2):
+            to_near(o, a).wait_send()
+            to_corner(o, a).wait_send()
         for k in range(4):
             to_sibling(o, k).wait_send()
 
@@ -627,8 +641,8 @@
     return pl.pallas_call(
         functools.partial(step_kernel, games),
         out_shape=(
-            jax.ShapeDtypeStruct((share + 8, CH), F32),
-            jax.ShapeDtypeStruct((2 * games + 8, 4 * CELLS), F32),
+            jax.ShapeDtypeStruct((share, CH), F32),
+            jax.ShapeDtypeStruct((2 * games, 4 * CELLS), F32),
         ),
         in_specs=[pl.BlockSpec(memory_space=pl.ANY) for _ in range(12)],
         out_specs=(vmem(), vmem()),
@@ -651,10 +665,12 @@
             dma((16,)),
             dma((3,)),
             dma((2,)),
-            dma((2, 3)),
+            dma((2, 2)),
+            dma((2, 2)),
             dma((2, 4)),
             dma((2, 4)),
-            dma((2, 4)),
+            dma((2, 2)),
+            dma((2, 2)),
             dma((12,)),
             dma,
             dma,
@@ -667,6 +683,32 @@
             collective_id=0, has_side_effects=True, vmem_limit_bytes=56 << 20
         ),
     )(boards, traj, *parts, torso, moment_one, moment_two)
+
+
+def finish_kernel(share, logp, share_out, logp_out, sems):
+    copies = [
+        pltpu.make_async_copy(share, share_out, sems.at[0]),
+        pltpu.make_async_copy(logp, logp_out, sems.at[1]),
+    ]
+    for copy in copies:
+        copy.start()
+    for copy in copies:
+        copy.wait()
+
+
+def finish(share, logp):
+    where = pl.BlockSpec(memory_space=pl.ANY)
+    return pl.pallas_call(
+        finish_kernel,
+        out_shape=(
+            jax.ShapeDtypeStruct(share.shape, F32),
+            jax.ShapeDtypeStruct(logp.shape, F32),
+        ),
+        in_specs=[where, where],
+        out_specs=(where, where),
+        scratch_shapes=[pltpu.SemaphoreType.DMA((2,))],
+        compiler_params=pltpu.CompilerParams(vmem_limit_bytes=60 << 20),
+    )(share, logp)
 
 
 def update_any(grad, torso, moment_one, moment_two):
@@ -734,8 +776,7 @@
     if lax.axis_size("dp") == 16 and lax.axis_size("role") == 2:
         parts = (policy_head.T, value_head[None, :], lengths[:, None])
         parts = parts + (actions, behaviour, regular, rewards)
-        new_share, logp = step_call(boards, traj, parts, torso, first_moment, second_moment)
-        return (new_share[: first_moment.shape[0]], logp[: board_now.shape[0]])
+        return finish(*step_call(boards, traj, parts, torso, first_moment, second_moment))
 
     def wide(x):
         return jnp.pad(x.astype(F32), ((0, 0), (0, CH - x.shape[1])))

time: 48.6 us -> 54 us (1.11)
  Pallas kernels: 44 us -> 52.6 us
  local copies, waits for them, and re-layouts: 3.09 us -> 0 us
    pallas_call x0 -> x1, Pallas kernels: none -> 7.32 us  [finish(): pl.pallas_call(finish_kernel, out_shape=(jax.ShapeDtypeStruct(share.shape...]
    slice x2 -> x0, local copies, waits for them, and re-layouts: 3.09 us -> none  [body(): return (new_share[:first_moment.shape[0]], logp[:board_now.shape[0]])]
    pallas_call x1, Pallas kernels: 44 us -> 45.2 us  [step_call(): pl.pallas_call(functools.partial(step_kernel, games), out_shape=(jax.Shap...]
where the time goes in v4:
time: 54 us; the launch traced here: 53.8 us
  Pallas kernels  52.6 us (97%)
  between operations  1.29 us (2%)
    pallas_call x1, Pallas kernels, step_call(): pl.pallas_call(functools.partial(step_kernel, games), out_shape=(jax.Shap...  45.2 us
    pallas_call x1, Pallas kernels, finish(): pl.pallas_call(finish_kernel, out_shape=(jax.ShapeDtypeStruct(share.shape...  7.32 us

profile of v4, /device:TPU:0, one launch (start us, length us, event | category | flops | bytes accessed | tf_op | source)
XLA Modules:
  0.0 53.8 jit_solution(1356918900803420760)
XLA Ops:
  1.3 45.2 %shard_map.131 = (f32[144,128]{1,0:T(8,128)}, f32[64,400]{1,0:T(8,128)}) custom-call(bf16[10,10,64,128]{3,2,1,0:T(8,128)(2,1)} %bitcast.8, bf16[10,10,16,128]{3,2,1,0:T(8,128)(2,1)} %bitcast.9, bf16[4,128]{1,0:T(4,128)(2,1)} %bitcast.10, bf16[1,128]{1,0:T(2,128)(2,1)} %bitcast.11, s32[1,1]{1,0:T(1,128)} %bitcast.7.refs_2_, s32[1,16]{1,0:T(1,128)} %refs_3_.1, ...), custom_call_target="tpu_custom_call" | custom-call | tf_op jit(solution)/shard_map/pallas_call | solution.py:641
  46.5 7.3 %shard_map.132 = (f32[144,128]{1,0:T(8,128)}, f32[64,400]{1,0:T(8,128)}) custom-call(f32[144,128]{1,0:T(8,128)} %get-tuple-element.4.share, f32[64,400]{1,0:T(8,128)} %get-tuple-element.5.logp), custom_call_target="tpu_custom_call" | custom-call | tf_op jit(solution)/shard_map/pallas_call | solution.py:701

commit v5 on v4

--- a/solution.py
+++ b/solution.py
@@ -357,9 +357,9 @@
 def step_kernel(games, boards, traj, *refs):
     parts, (torso, moment_one, moment_two, share_out, out), scratch = refs[:7], refs[7:12], refs[12:]
     (weights, full, torso_in, one_in, two_in, grad, plane, quarter, line, norms) = scratch[:10]
-    (s1, r1, s2, r2, sn, rn, sz, rz, sp, rp, ss, rs, sc, rc, loads, send_out, recv_out) = scratch[10:27]
-    learner_refs, actor_refs = scratch[27:35], scratch[35:39]
-    given, part_refs = scratch[39], scratch[40:]
+    (s1, r1, s2, r2, sn, rn, sz, rz, sp, rp, ss, rs, loads, send_out, recv_out) = scratch[10:25]
+    learner_refs, actor_refs = scratch[25:33], scratch[33:37]
+    given, part_refs = scratch[37], scratch[38:]
     share = moment_one.shape[0]
     role = lax.axis_index("role")
     dp = lax.axis_index("dp")
@@ -494,33 +494,20 @@
         def _():
             to_owner(o).start()
 
-    half = share // 2
-    near = (spot + 1 - 2 * (spot % 2), (spot + 2) % 4)
-    places = (spot,) + near + (3 - spot,)
+    others = tuple((spot + k) % 4 for k in range(1, 4))
+    places = (spot,) + others
 
     def share_of(o, place, to_role=None):
         group = role if to_role is None else to_role
         return full.at[rows((2 * group + o) * 4 + place)]
 
-    def half_of(o, place, part):
-        begin = ((2 * role + o) * 4 + place) * share + part * half
-        return full.at[pl.ds(pl.multiple_of(begin, 8), half)]
-
     def to_near(o, a):
         at = share_of(o, spot)
-        return send(at, at, sp.at[o, a], rp.at[o, a], role, z * 4 + near[a])
+        return send(at, at, sp.at[o, a], rp.at[o, 2 - a], role, z * 4 + others[a])
 
     def from_near(o, a):
-        at = share_of(o, near[a])
-        return send(at, at, sp.at[o, a], rp.at[o, a], role, z * 4 + near[a])
-
-    def to_corner(o, a):
-        at = half_of(o, near[a], a)
-        return send(at, at, sc.at[o, a], rc.at[o, a], role, z * 4 + near[1 - a])
-
-    def from_corner(o, a):
-        at = half_of(o, 3 - spot, a)
-        return send(at, at, sc.at[o, a], rc.at[o, a], role, z * 4 + near[1 - a])
+        at = share_of(o, others[a])
+        return send(at, at, sp.at[o, a], rp.at[o, a], role, z * 4 + others[a])
 
     def to_sibling(o, n):
         at = share_of(o, places[n])
@@ -568,7 +555,7 @@
         full[rows(dp)] = torso_in[rows(dp)] - LEARN_RATE * one / (jnp.sqrt(two) + ADAM_EPS)
         for k in range(1, 4):
             down_line(k).start()
-        for a in range(2):
+        for a in range(3):
             to_near(z % 2, a).start()
         to_sibling(z % 2, 0).start()
 
@@ -580,48 +567,18 @@
         def _():
             at = share_of(o, spot)
             send(at, at, sz.at[0], rz.at[o], role, (2 * role + o) * 4 + spot).wait_recv()
-            for a in range(2):
+            for a in range(3):
                 to_near(o, a).start()
             to_sibling(o, 0).start()
 
     for o in (first, 1 - first):
-        for a in range(2):
+        for a in range(3):
             from_near(o, a).wait_recv()
-            to_corner(o, a).start()
             to_sibling(o, 1 + a).start()
-    for o in (first, 1 - first):
-        for a in range(2):
-            from_corner(o, a).wait_recv()
-        to_sibling(o, 3).start()
-
-    def from_sibling():
-        for o in range(2):
-            for n in range(4):
-                at = share_of(o, places[n], 1 - role)
-                send(at, at, ss.at[o, n], rs.at[o, n], 1 - role, dp).wait_recv()
-
-    def ready(layer):
-        @pl.when(role == 1 - layer)
-        def _():
-            from_sibling()
-
-        pack_layer(weights, full, layer)
-
-    actor_part(given, weights, actor_refs, games, out, start, ready)
-    share_out[...] = full[rows(dp)]
-    mine = out.at[pl.ds(start, games)]
-    send(mine, mine, send_out, recv_out, 1 - role, dp).start()
-    theirs = out.at[pl.ds(pl.multiple_of((1 - role) * games, games), games)]
-    send(mine, theirs, send_out, recv_out, 1 - role, dp).wait_recv()
-    send(mine, mine, send_out, recv_out, 1 - role, dp).wait_send()
+
     for o in range(2):
         for k in range(1, 4):
             to_plane(o, k).wait_send()
-        for a in range(2):
-            to_near(o, a).wait_send()
-            to_corner(o, a).wait_send()
-        for k in range(4):
-            to_sibling(o, k).wait_send()
 
         @pl.when(z != 2 * role + o)
         def _():
@@ -633,6 +590,32 @@
             to_norm(k).wait_send()
         for k in range(1, 4):
             down_line(k).wait_send()
+
+    def from_sibling():
+        for o in range(2):
+            for n in range(4):
+                at = share_of(o, places[n], 1 - role)
+                send(at, at, ss.at[o, n], rs.at[o, n], 1 - role, dp).wait_recv()
+
+    def ready(layer):
+        @pl.when(role == 1 - layer)
+        def _():
+            from_sibling()
+
+        pack_layer(weights, full, layer)
+
+    actor_part(given, weights, actor_refs, games, out, start, ready)
+    mine = out.at[pl.ds(start, games)]
+    send(mine, mine, send_out, recv_out, 1 - role, dp).start()
+    share_out[...] = full[rows(dp)]
+    for o in range(2):
+        for a in range(3):
+            to_near(o, a).wait_send()
+        for n in range(4):
+            to_sibling(o, n).wait_send()
+    theirs = out.at[pl.ds(pl.multiple_of((1 - role) * games, games), games)]
+    send(mine, theirs, send_out, recv_out, 1 - role, dp).wait_recv()
+    send(mine, mine, send_out, recv_out, 1 - role, dp).wait_send()
 
 
 def step_call(boards, traj, parts, torso, moment_one, moment_two):
@@ -665,12 +648,10 @@
             dma((16,)),
             dma((3,)),
             dma((2,)),
-            dma((2, 2)),
-            dma((2, 2)),
+            dma((2, 3)),
+            dma((2, 3)),
             dma((2, 4)),
             dma((2, 4)),
-            dma((2, 2)),
-            dma((2, 2)),
             dma((12,)),
             dma,
             dma,
@@ -685,15 +666,22 @@
     )(boards, traj, *parts, torso, moment_one, moment_two)
 
 
-def finish_kernel(share, logp, share_out, logp_out, sems):
-    copies = [
-        pltpu.make_async_copy(share, share_out, sems.at[0]),
-        pltpu.make_async_copy(logp, logp_out, sems.at[1]),
+def finish_kernel(share, logp, share_out, logp_out, share_at, logp_at, sems):
+    reads = [
+        pltpu.make_async_copy(share, share_at, sems.at[0]),
+        pltpu.make_async_copy(logp, logp_at, sems.at[1]),
     ]
-    for copy in copies:
-        copy.start()
-    for copy in copies:
-        copy.wait()
+    writes = [
+        pltpu.make_async_copy(share_at, share_out, sems.at[2]),
+        pltpu.make_async_copy(logp_at, logp_out, sems.at[3]),
+    ]
+    for read in reads:
+        read.start()
+    for read, write in zip(reads, writes):
+        read.wait()
+        write.start()
+    for write in writes:
+        write.wait()
 
 
 def finish(share, logp):
@@ -706,7 +694,11 @@
         ),
         in_specs=[where, where],
         out_specs=(where, where),
-        scratch_shapes=[pltpu.SemaphoreType.DMA((2,))],
+        scratch_shapes=[
+            pltpu.VMEM(share.shape, F32),
+            pltpu.VMEM(logp.shape, F32),
+            pltpu.SemaphoreType.DMA((4,)),
+        ],
         compiler_params=pltpu.CompilerParams(vmem_limit_bytes=60 << 20),
     )(share, logp)
 

time: 54 us -> 47.1 us (0.87)
  Pallas kernels: 52.6 us -> 45.6 us
    pallas_call x1, Pallas kernels: 7.32 us -> 1.63 us  [finish(): pl.pallas_call(finish_kernel, out_shape=(jax.ShapeDtypeStruct(share.shape...]
    pallas_call x1, Pallas kernels: 45.2 us -> 44 us  [step_call(): pl.pallas_call(functools.partial(step_kernel, games), out_shape=(jax.Shap...]
where the time goes in v5:
time: 47.1 us; the launch traced here: 46.9 us
  Pallas kernels  45.6 us (97%)
  between operations  1.29 us (3%)
    pallas_call x1, Pallas kernels, step_call(): pl.pallas_call(functools.partial(step_kernel, games), out_shape=(jax.Shap...  44 us
    pallas_call x1, Pallas kernels, finish(): pl.pallas_call(finish_kernel, out_shape=(jax.ShapeDtypeStruct(share.shape...  1.63 us

profile of v5, /device:TPU:0, one launch (start us, length us, event | category | flops | bytes accessed | tf_op | source)
XLA Modules:
  0.0 46.9 jit_solution(16449807376776682555)
XLA Ops:
  1.3 44.0 %shard_map.131 = (f32[144,128]{1,0:T(8,128)}, f32[64,400]{1,0:T(8,128)}) custom-call(bf16[10,10,64,128]{3,2,1,0:T(8,128)(2,1)} %bitcast.8, bf16[10,10,16,128]{3,2,1,0:T(8,128)(2,1)} %bitcast.9, bf16[4,128]{1,0:T(4,128)(2,1)} %bitcast.10, bf16[1,128]{1,0:T(2,128)(2,1)} %bitcast.11, s32[1,1]{1,0:T(1,128)} %bitcast.7.refs_2_, s32[1,16]{1,0:T(1,128)} %refs_3_.1, ...), custom_call_target="tpu_custom_call" | custom-call | tf_op jit(solution)/shard_map/pallas_call | solution.py:624
  45.3 1.6 %shard_map.132 = (f32[144,128]{1,0:T(8,128)}, f32[64,400]{1,0:T(8,128)}) custom-call(f32[144,128]{1,0:T(8,128)} %get-tuple-element.4.share, f32[64,400]{1,0:T(8,128)} %get-tuple-element.5.logp), custom_call_target="tpu_custom_call" | custom-call | tf_op jit(solution)/shard_map/pallas_call | solution.py:689

commit v6 on v5

--- a/solution.py
+++ b/solution.py
@@ -189,6 +189,14 @@
         set_inner(h1, i, games, h)
 
     steps(layer_one)
+    pack_layer(weights, torso, 1)
+    turned[...] = jnp.zeros(turned.shape, BF16)
+
+    def block(offset):
+        at = TAPS + offset * CH
+        return torso[at : at + CH, :].T.astype(BF16)
+
+    pack(turned, block, True)
 
     def layer_two(step, i):
         act, h = advance(h1, i, games, weights.at[1])
@@ -213,14 +221,6 @@
 
     @pl.when(role == 0)
     def _():
-        turned[...] = jnp.zeros(turned.shape, BF16)
-
-        def block(offset):
-            at = TAPS + offset * CH
-            return torso[at : at + CH, :].T.astype(BF16)
-
-        pack(turned, block, True)
-
         def back(step, i):
             at = pl.ds(step * size, size)
             out = hidden_grad[at] + pair_dot(a1, i, games, turned[...])
@@ -310,8 +310,7 @@
     copy = pltpu.make_async_copy(traj, center(hs.at[0]), sem)
     copy.start()
     weights[...] = jnp.zeros(weights.shape, BF16)
-    for layer in range(2):
-        pack_layer(weights, torso, layer)
+    pack_layer(weights, torso, 0)
     copy.wait()
     learner_part(given, torso, grad, weights, scratch, lambda half: None)
 
@@ -435,8 +434,7 @@
         given[8 + n : 9 + n, 0:16] = ref[...].astype(F32)
     weights[...] = jnp.zeros(weights.shape, BF16)
     load_torso.wait()
-    for layer in range(2):
-        pack_layer(weights, torso_in, layer)
+    pack_layer(weights, torso_in, 0)
     load_traj.wait()
 
     def rows(index):

time: 47.1 us -> 46.9 us (level)
  no operation moved by 1% of the time
where the time goes in v6:
time: 46.9 us; the launch traced here: 46.7 us
  Pallas kernels  45.4 us (97%)
  between operations  1.29 us (3%)
    pallas_call x1, Pallas kernels, step_call(): pl.pallas_call(functools.partial(step_kernel, games), out_shape=(jax.Shap...  43.8 us
    pallas_call x1, Pallas kernels, finish(): pl.pallas_call(finish_kernel, out_shape=(jax.ShapeDtypeStruct(share.shape...  1.63 us

profile of v6, /device:TPU:0, one launch (start us, length us, event | category | flops | bytes accessed | tf_op | source)
XLA Modules:
  0.0 46.7 jit_solution(8467725226714123342)
XLA Ops:
  1.3 43.8 %shard_map.131 = (f32[144,128]{1,0:T(8,128)}, f32[64,400]{1,0:T(8,128)}) custom-call(bf16[10,10,64,128]{3,2,1,0:T(8,128)(2,1)} %bitcast.8, bf16[10,10,16,128]{3,2,1,0:T(8,128)(2,1)} %bitcast.9, bf16[4,128]{1,0:T(4,128)(2,1)} %bitcast.10, bf16[1,128]{1,0:T(2,128)(2,1)} %bitcast.11, s32[1,1]{1,0:T(1,128)} %bitcast.7.refs_2_, s32[1,16]{1,0:T(1,128)} %refs_3_.1, ...), custom_call_target="tpu_custom_call" | custom-call | tf_op jit(solution)/shard_map/pallas_call | solution.py:622
  45.1 1.6 %shard_map.132 = (f32[144,128]{1,0:T(8,128)}, f32[64,400]{1,0:T(8,128)}) custom-call(f32[144,128]{1,0:T(8,128)} %get-tuple-element.4.share, f32[64,400]{1,0:T(8,128)} %get-tuple-element.5.logp), custom_call_target="tpu_custom_call" | custom-call | tf_op jit(solution)/shard_map/pallas_call | solution.py:687
